TPU v7x, 32 devices: a whole 2x2x4 slice. The times are simulated.
32 devices in a mesh: ty: 8 (over y, x, core), tx: 4 (over z).
Axes of the slice: x: 2, y: 2, z: 4, core: 2. Of those that a mesh axis runs over, the one named last changes fastest.
Arguments:
- object_field: float32 [2, 4096, 2048], P(None, 'ty', 'tx'), may hold values from -5 to 5
- probe_field: float32 [2, 128, 128], replicated, may hold values from -5 to 5
- owners: int32 [2, 768, 1], P(None, ('ty', 'tx')), may hold values from 0 to 7; in each aligned block of 24 rows (0 to 23, 24 to 47, ..., all dimensions but the last counted through in order) at most 3 rows name the same one
- row_offsets: int32 [2, 768], P(None, ('ty', 'tx')), may hold values from 0 to 511
- col_offsets: int32 [2, 768], P(None, ('ty', 'tx')), may hold values from 0 to 511
- intensities: float32 [2, 768, 128, 128], P(None, ('ty', 'tx')), may hold values from 0.1 to 3
Outputs:
- new_object: float32 [2, 4096, 2048], P(None, 'ty', 'tx')
- new_probe: float32 [2, 128, 128], replicated
Inputs may be any that keep to these rules, and one draw needn't show every extreme that they name: `owners`: in each step the 24 positions of one device name each band at most 3 times; some device names some band exactly 3 times.
All inputs are finite; a program needn't handle non-finite values.
Results may differ from a plain program's by a relative error of at most 0.00022.
Values sent between devices are 32-bit elements; how exact they have to be, the bound alone decides.
A program may use at most 128 MiB of HBM per device.

v0:
```python
import math

import jax
import jax.numpy as jnp
from jax import lax
from jax.sharding import PartitionSpec as P

CAP = 3
STEPS = 2


OBJECT_RATE = 0.25
PROBE_RATE = 1.0
HIGHEST = lax.Precision.HIGHEST


def shifted(value, axis, steps):
    count = lax.axis_size(axis)
    leading, last = (max(0, -steps), min(count, count - steps))
    return lax.ppermute(value, axis, [(source, source + steps) for source in range(leading, last)])


def dft_tables(width):
    counter = jnp.arange(width, dtype=jnp.int32)
    product = counter[:, None] * counter[None, :] % width
    radians = product.astype(jnp.float32) * (2.0 * math.pi / width)
    factor = 1.0 / math.sqrt(width)
    return (jnp.cos(radians) * factor, -jnp.sin(radians) * factor)


def left_apply(table_re, table_im, data_re, data_im):

    def product_of(table, data):
        return jnp.einsum("kn,bnm->bkm", table, data, precision=HIGHEST)

    return (
        product_of(table_re, data_re) - product_of(table_im, data_im),
        product_of(table_re, data_im) + product_of(table_im, data_re),
    )


def right_apply(data_re, data_im, table_re, table_im):

    def product_of(data, table):
        return jnp.einsum("bkn,nm->bkm", data, table, precision=HIGHEST)

    return (
        product_of(data_re, table_re) - product_of(data_im, table_im),
        product_of(data_im, table_re) + product_of(data_re, table_im),
    )


def pattern_terms(patches, probe_field, measured, weights, tables):
    cos_table, sin_table = tables
    patch_re = patches[:, 0]
    patch_im = patches[:, 1]
    probe_re = probe_field[0][None]
    probe_im = probe_field[1][None]
    wave_re = probe_re * patch_re - probe_im * patch_im
    wave_im = probe_re * patch_im + probe_im * patch_re
    half_re, half_im = left_apply(cos_table, sin_table, wave_re, wave_im)
    far_re, far_im = right_apply(half_re, half_im, cos_table, sin_table)
    misfit = (far_re * far_re + far_im * far_im - measured) * weights[:, None, None]
    half_re, half_im = left_apply(cos_table, -sin_table, misfit * far_re, misfit * far_im)
    back_re, back_im = right_apply(half_re, half_im, cos_table, -sin_table)
    object_terms = jnp.stack(
        [probe_re * back_re + probe_im * back_im, probe_re * back_im - probe_im * back_re], axis=1
    )
    probe_term = jnp.stack(
        [
            jnp.sum(patch_re * back_re + patch_im * back_im, axis=0),
            jnp.sum(patch_re * back_im - patch_im * back_re, axis=0),
        ]
    )
    return (object_terms, probe_term)


def extend_tile(object_field, width):
    right_part = shifted(object_field[:, :, :width], "tx", -1)
    widened = jnp.concatenate([object_field, right_part], axis=2)
    lower_part = shifted(widened[:, :width, :], "ty", -1)
    return jnp.concatenate([widened, lower_part], axis=1)


def cut_patches(extended, tops, lefts, width):
    anchor = jnp.zeros((), jnp.int32)

    def cut_one(top_row, left_col):
        return lax.dynamic_slice(extended, (anchor, top_row, left_col), (2, width, width))

    return jax.vmap(cut_one)(tops, lefts)


def accumulate(extended_shape, terms, tops, lefts, width):
    anchor = jnp.zeros((), jnp.int32)

    def add_slot(slot_number, total):
        corner = (anchor, tops[slot_number], lefts[slot_number])
        present_block = lax.dynamic_slice(total, corner, (2, width, width))
        return lax.dynamic_update_slice(total, present_block + terms[slot_number], corner)

    return lax.fori_loop(0, terms.shape[0], add_slot, jnp.zeros(extended_shape, jnp.float32))


def fold_back(total, tile_rows, tile_cols, width):
    spill_down = shifted(total[:, tile_rows:, :], "ty", 1)
    upper_part = total[:, :tile_rows, :]
    upper_part = jnp.concatenate(
        [upper_part[:, :width, :] + spill_down, upper_part[:, width:, :]], axis=1
    )
    spill_right = shifted(upper_part[:, :, tile_cols:], "tx", 1)
    return jnp.concatenate(
        [upper_part[:, :, :width] + spill_right, upper_part[:, :, width:tile_cols]], axis=2
    )


def on_device(object_field, probe_field, owners, row_offsets, col_offsets, intensities):
    band_count = lax.axis_size("ty")
    strip_count = lax.axis_size("tx")
    tile_rows = object_field.shape[1]
    tile_cols = object_field.shape[2]
    width = probe_field.shape[1]
    batch_rows = row_offsets.shape[1]
    slot_count = band_count * CAP
    strip_index = lax.axis_index("tx")
    tables = dft_tables(width)
    position_ids = jnp.arange(batch_rows, dtype=jnp.int32)
    slot_ids = jnp.arange(slot_count, dtype=jnp.int32)
    probe_scale = PROBE_RATE / (batch_rows * band_count * strip_count)
    for step_number in range(STEPS):
        extended = extend_tile(object_field, width)
        owner_rows = owners[step_number, :, 0]
        earlier = (owner_rows[None, :] == owner_rows[:, None]) & (
            position_ids[None, :] < position_ids[:, None]
        )
        rank_among = jnp.sum(earlier.astype(jnp.int32), axis=1)
        slot_of = owner_rows * CAP + rank_among
        top_local = (
            jnp.minimum(
                owner_rows * tile_rows + row_offsets[step_number], tile_rows * band_count - width
            )
            - owner_rows * tile_rows
        )
        left_local = (
            jnp.minimum(
                strip_index * tile_cols + col_offsets[step_number], tile_cols * strip_count - width
            )
            - strip_index * tile_cols
        )
        matches = slot_of[None, :] == slot_ids[:, None]
        filled = jnp.any(matches, axis=1)
        want_top = jnp.where(filled, jnp.sum(jnp.where(matches, top_local[None, :], 0), axis=1), -1)
        want_left = jnp.where(
            filled, jnp.sum(jnp.where(matches, left_local[None, :], 0), axis=1), 0
        )
        wanted = jnp.stack([want_top, want_left]).reshape(2, band_count, CAP)
        received = lax.all_to_all(wanted, "ty", split_axis=1, concat_axis=1, tiled=True).reshape(
            2, slot_count
        )
        patches = cut_patches(extended, received[0], received[1], width)
        patches = lax.all_to_all(
            patches.reshape(band_count, CAP, 2, width, width),
            "ty",
            split_axis=0,
            concat_axis=0,
            tiled=True,
        )
        chosen = jnp.take(patches.reshape(slot_count, 2, width, width), slot_of, axis=0)
        terms, probe_term = pattern_terms(
            chosen,
            probe_field,
            intensities[step_number],
            jnp.ones((batch_rows,), jnp.float32),
            tables,
        )
        placed = jnp.zeros((slot_count, 2, width, width), jnp.float32).at[slot_of].set(terms)
        returned = lax.all_to_all(
            placed.reshape(band_count, CAP, 2, width, width),
            "ty",
            split_axis=0,
            concat_axis=0,
            tiled=True,
        )
        returned = returned.reshape(slot_count, 2, width, width)
        gathered = accumulate(extended.shape, returned, received[0], received[1], width)
        gradient = fold_back(gathered, tile_rows, tile_cols, width)
        probe_total = lax.psum(probe_term, ("ty", "tx"))
        object_field = object_field - OBJECT_RATE * gradient
        probe_field = probe_field - probe_scale * probe_total
    return (object_field, probe_field)


def solution(mesh):
    in_specs = (
        P(None, "ty", "tx"),
        P(),
        P(None, ("ty", "tx"), None),
        P(None, ("ty", "tx")),
        P(None, ("ty", "tx")),
        P(None, ("ty", "tx"), None, None),
    )
    out_specs = (P(None, "ty", "tx"), P())
    return jax.shard_map(
        on_device, mesh=mesh, in_specs=in_specs, out_specs=out_specs, check_vma=False
    )
```

profile of v0, /device:TPU:3, one launch (start us, length us, event | category | flops | bytes accessed | tf_op | source)
XLA Modules:
  0.0 1290.3 jit_solution(10855963669126769437)
XLA Ops:
  12.0 4.6 all-to-all-start
  28.9 4.7 collective-permute-done
  37.9 9.7 collective-permute-done.1
  49.8 74.3 %while.30 = (s32[]{:T(128)}, f32[2,640,640]{2,1,0:T(8,128)}, s32[24,3]{0,1:T(4,128)S(1)}, f32[24,2,128,128]{3,2,1,0:T(8,128)S(1)}, s32[]{:T(128)}) while((s32[]{:T(128)}, f32[2,640,640]{2,1,0:T(8,128)}, s32[24,3]{0,1:T(4,128)S(1)}, f32[24,2,128,128]{3,2,1,0:T(8,128)S(1)}, s32[]{:T(128)}) %tuple.117), condition=%wide.while_cond, body=%wide.while_body.sunk | while | flops 2 | bytes 262261 | solution.py:89
  130.4 34.7 %all-to-all-done.1 = f32[8,3,2,128,128]{4,3,2,1,0:T(8,128)S(1)} async-done(((f32[8,3,2,128,128]{4,3,2,1,0:T(8,128)}), f32[8,3,2,128,128]{4,3,2,1,0:T(8,128)S(1)}, u32[]{:S(2)}, u32[]{:S(2)}) %all-to-all-start.1) | async-done | bytes 3145760 | tf_op jit(solution)/shard_map/all_to_all | solution.py:161
  222.2 7.8 scatter_fusion
  230.1 6.3 all-to-all-start.2
  237.5 35.2 %all-to-all-done.2 = f32[8,3,2,128,128]{4,3,2,1,0:T(8,128)} async-done(((f32[8,3,2,128,128]{4,3,2,1,0:T(8,128)}), f32[8,3,2,128,128]{4,3,2,1,0:T(8,128)}, u32[]{:S(2)}, u32[]{:S(2)}) %all-to-all-start.2) | async-done | bytes 3145760 | tf_op jit(solution)/shard_map/all_to_all | solution.py:177
  274.6 265.5 %while.28 = (s32[]{:T(128)}, f32[2,640,640]{2,1,0:T(8,128)}, s32[24]{0:T(128)}, s32[24]{0:T(128)}, f32[24,2,128,128]{3,2,1,0:T(8,128)}, /*index=5*/s32[]{:T(128)}, s32[]{:T(128)}, s32[]{:T(128)}) while((s32[]{:T(128)}, f32[2,640,640]{2,1,0:T(8,128)}, s32[24]{0:T(128)}, s32[24]{0:T(128)}, f32[24,2,128,128]{3,2,1,0:T(8,128)}, ...), condition=%wide.region_6.8_spmd, body=%wide.region_5.7_spmd.sunk | while | flops 32776 | bytes 655553 | solution.py:102
  546.4 5.8 collective-permute-done.2
  556.5 10.2 collective-permute-done.3
  568.6 13.1 %collective-permute-done.4 = f32[2,512,128]{2,1,0:T(8,128)S(1)} collective-permute-done((f32[2,512,128]{2,1,0:T(8,128)S(1)}, f32[2,512,128]{2,1,0:T(8,128)S(1)}, u32[]{:S(2)}, u32[]{:S(2)}) %collective-permute-start.4) | collective-permute-done | bytes 524320 | tf_op jit(solution)/shard_map/ppermute | solution.py:20
  582.7 4.4 collective-permute-start.5
  587.1 8.7 collective-permute-done.5
  601.7 86.4 %while.31 = (s32[]{:T(128)}, f32[2,640,640]{2,1,0:T(8,128)}, s32[24,3]{0,1:T(4,128)S(1)}, f32[24,2,128,128]{3,2,1,0:T(8,128)}, s32[]{:T(128)}) while((s32[]{:T(128)}, f32[2,640,640]{2,1,0:T(8,128)}, s32[24,3]{0,1:T(4,128)S(1)}, f32[24,2,128,128]{3,2,1,0:T(8,128)}, s32[]{:T(128)}) %tuple.123), condition=%wide.while_cond.1, body=%wide.while_body.1.sunk | while | flops 2 | bytes 263785 | solution.py:89
  688.2 4.5 all-to-all-start.4
  693.7 130.8 %all-reduce.3.cloned.1.call-done = f32[2,128,128]{2,1,0:T(8,128)} async-done(((f32[2,128,128]{2,1,0:T(8,128)}), f32[2,128,128]{2,1,0:T(8,128)}) %all-reduce.3.cloned.1.call-update) | async-done | bytes 131088 | tf_op jit(solution)/shard_map/psum | solution.py:187
  883.1 7.0 scatter_fusion.1
  890.1 5.1 all-to-all-start.5
  895.4 36.1 %all-to-all-done.5 = f32[8,3,2,128,128]{4,3,2,1,0:T(8,128)S(1)} async-done(((f32[8,3,2,128,128]{4,3,2,1,0:T(8,128)}), f32[8,3,2,128,128]{4,3,2,1,0:T(8,128)S(1)}, u32[]{:S(2)}, u32[]{:S(2)}) %all-to-all-start.5) | async-done | bytes 3145760 | tf_op jit(solution)/shard_map/all_to_all | solution.py:177
  933.4 204.1 %while.29 = (s32[]{:T(128)}, f32[2,640,640]{2,1,0:T(8,128)S(1)}, s32[24]{0:T(128)S(1)}, s32[24]{0:T(128)S(1)}, f32[24,2,128,128]{3,2,1,0:T(8,128)}, /*index=5*/s32[]{:T(128)}, s32[]{:T(128)}, s32[]{:T(128)}) while((s32[]{:T(128)}, f32[2,640,640]{2,1,0:T(8,128)S(1)}, s32[24]{0:T(128)S(1)}, s32[24]{0:T(128)S(1)}, ...), condition=%wide.region_16.18_spmd, body=%wide.region_15.17_spmd.sunk | while | flops 32776 | bytes 655553 | solution.py:102
  1139.2 5.1 collective-permute-start.6
  1146.0 5.8 collective-permute-done.6
  1157.1 121.3 %all-reduce.5.cloned.1.call-done = f32[2,128,128]{2,1,0:T(8,128)} async-done(((f32[2,128,128]{2,1,0:T(8,128)}), f32[2,128,128]{2,1,0:T(8,128)}) %all-reduce.5.cloned.1.call-update) | async-done | bytes 131088 | tf_op jit(solution)/shard_map/psum | solution.py:187
  (500 shorter events, 630.6 us)
Async XLA Ops:
  10.2 16.5 %copy-start.16 = (s32[24]{0:T(128)}, s32[24]{0:T(128)S(1)}, u32[]{:S(2)}) copy-start(s32[24]{0:T(128)S(1)} %get-tuple-element.258) | copy-start | bytes 292
  12.0 8.8 all-to-all-start
  18.4 15.2 %collective-permute-start = (f32[2,512,128]{2,1,0:T(8,128)}, f32[2,512,128]{2,1,0:T(8,128)S(1)}, u32[]{:S(2)}, u32[]{:S(2)}) collective-permute-start(f32[2,512,128]{2,1,0:T(8,128)} %slice.128), channel_id=1, source_target_pairs={{1,0},{2,1},{3,2},{5,4},{6,5},{7,6},{9,8},{10,9},{11,10},{13,12},{... | collective-permute-start | bytes 1572872 | tf_op jit(solution)/shard_map/ppermute | solution.py:20
  20.7 7.4 all-to-all-start.3
  34.6 13.0 %collective-permute-start.1 = (f32[2,128,640]{2,1,0:T(8,128)}, f32[2,128,640]{2,1,0:T(8,128)S(1)}, u32[]{:S(2)}, u32[]{:S(2)}) collective-permute-start(f32[2,128,640]{2,1,0:T(8,128)} %slice.194), channel_id=1, source_target_pairs={{4,0},{8,4},{12,8},{16,12},{20,16},{24,20},{28,24},{5,1},{9,5},{13... | collective-permute-start | bytes 1966088 | tf_op jit(solution)/shard_map/ppermute | solution.py:20
  125.8 4.1 copy-start.12
  125.8 4.6 copy-start.8
  125.8 39.3 %all-to-all-start.1 = ((f32[8,3,2,128,128]{4,3,2,1,0:T(8,128)}), f32[8,3,2,128,128]{4,3,2,1,0:T(8,128)S(1)}, u32[]{:S(2)}, u32[]{:S(2)}) async-start(f32[8,3,2,128,128]{4,3,2,1,0:T(8,128)} %bitcast.333), calls=%async_computation.1 | async-start | bytes 6291456 | tf_op jit(solution)/shard_map/all_to_all | solution.py:161
  230.1 6.3 copy-start.11
  230.1 42.7 %all-to-all-start.2 = ((f32[8,3,2,128,128]{4,3,2,1,0:T(8,128)}), f32[8,3,2,128,128]{4,3,2,1,0:T(8,128)}, u32[]{:S(2)}, u32[]{:S(2)}) async-start(f32[8,3,2,128,128]{4,3,2,1,0:T(8,128)} %bitcast.331), calls=%async_computation.2 | async-start | bytes 6291456 | tf_op jit(solution)/shard_map/all_to_all | solution.py:177
  541.2 10.9 collective-permute-start.2
  553.4 13.4 %copy-start.5 = (f32[2,512,512]{2,1,0:T(8,128)S(1)}, f32[2,512,512]{2,1,0:T(8,128)}, u32[]{:S(2)}) copy-start(f32[2,512,512]{2,1,0:T(8,128)} %param.12) | copy-start | bytes 6291460
  553.4 13.3 %collective-permute-start.3 = (f32[2,512,128]{2,1,0:T(8,128)S(1)}, f32[2,512,128]{2,1,0:T(8,128)S(1)}, u32[]{:S(2)}, u32[]{:S(2)}) collective-permute-start(f32[2,512,128]{2,1,0:T(8,128)S(1)} %pad_maximum_fusion.6), channel_id=1, source_target_pairs={{0,1},{1,2},{2,3},{4,5},{5,6},{6,7},{8,9},{9,10},{10,11},{12,13},{... | collective-permute-start | bytes 1572872 | tf_op jit(solution)/shard_map/ppermute | solution.py:20
  567.2 15.5 %copy-start.1 = (f32[2,512,512]{2,1,0:T(8,128)}, f32[2,512,512]{2,1,0:T(8,128)S(1)}, u32[]{:S(2)}) copy-start(f32[2,512,512]{2,1,0:T(8,128)S(1)} %fusion.5) | copy-start | bytes 6291460
  567.3 14.4 %collective-permute-start.4 = (f32[2,512,128]{2,1,0:T(8,128)S(1)}, f32[2,512,128]{2,1,0:T(8,128)S(1)}, u32[]{:S(2)}, u32[]{:S(2)}) collective-permute-start(f32[2,512,128]{2,1,0:T(8,128)S(1)} %slice.200), channel_id=1, source_target_pairs={{1,0},{2,1},{3,2},{5,4},{6,5},{7,6},{9,8},{10,9},{11,10},{13,12},{... | collective-permute-start | bytes 1572872 | tf_op jit(solution)/shard_map/ppermute | solution.py:20
  582.7 13.1 %collective-permute-start.5 = (f32[2,128,640]{2,1,0:T(8,128)}, f32[2,128,640]{2,1,0:T(8,128)}, u32[]{:S(2)}, u32[]{:S(2)}) collective-permute-start(f32[2,128,640]{2,1,0:T(8,128)} %pad_maximum_fusion.4), channel_id=1, source_target_pairs={{4,0},{8,4},{12,8},{16,12},{20,16},{24,20},{28,24},{5,1},{9,5},{13... | collective-permute-start | bytes 1966088 | tf_op jit(solution)/shard_map/ppermute | solution.py:20
  688.2 4.8 copy-start.17
  688.2 137.2 %all-to-all-start.4 = ((f32[8,3,2,128,128]{4,3,2,1,0:T(8,128)}), f32[8,3,2,128,128]{4,3,2,1,0:T(8,128)}, u32[]{:S(2)}, u32[]{:S(2)}) async-start(f32[8,3,2,128,128]{4,3,2,1,0:T(8,128)} %bitcast.334), calls=%async_computation.4 | async-start | bytes 6291456 | tf_op jit(solution)/shard_map/all_to_all | solution.py:161
  692.7 131.7 %all-reduce.3.cloned.1.call-start = ((), (), s32[]{:S(2)}) async-start(), calls=%async_computation.6 | async-start | bytes 262144 | tf_op jit(solution)/shard_map/psum | solution.py:187
  825.4 4.3 copy-start.15
  890.1 41.4 %all-to-all-start.5 = ((f32[8,3,2,128,128]{4,3,2,1,0:T(8,128)}), f32[8,3,2,128,128]{4,3,2,1,0:T(8,128)S(1)}, u32[]{:S(2)}, u32[]{:S(2)}) async-start(f32[8,3,2,128,128]{4,3,2,1,0:T(8,128)} %bitcast.53), calls=%async_computation.5 | async-start | bytes 6291456 | tf_op jit(solution)/shard_map/all_to_all | solution.py:177
  895.2 383.2 %all-reduce.5.cloned.1.call-start = ((), (), s32[]{:S(2)}) async-start(), calls=%async_computation.7 | async-start | bytes 262144 | tf_op jit(solution)/shard_map/psum | solution.py:187
  1139.2 12.6 collective-permute-start.6
  1153.8 126.2 %collective-permute-start.7 = (f32[2,512,128]{2,1,0:T(8,128)}, f32[2,512,128]{2,1,0:T(8,128)S(1)}, u32[]{:S(2)}, u32[]{:S(2)}) collective-permute-start(f32[2,512,128]{2,1,0:T(8,128)} %pad_maximum_fusion.5), channel_id=1, source_target_pairs={{0,1},{1,2},{2,3},{4,5},{5,6},{6,7},{8,9},{9,10},{10,11},{12,13},{... | collective-permute-start | bytes 1572872 | tf_op jit(solution)/shard_map/ppermute | solution.py:20
  (10 other events, 21.2 us)
Sparse Core Ops, SparseCore 0:
  699.7 124.7 all-reduce.2
  1157.2 121.1 all-reduce.4
where the time goes:
time: 1300 us; the launch traced here: 1290 us
  local copies, waits for them, and re-layouts  447 us (34%)
  waiting for transfers between devices  418 us (32%)
  loops' own time  184 us (14%)
  matrix products  96.8 us (7%)
  other arithmetic  76.8 us (6%)
  starting transfers between devices  53.1 us (4%)
  between operations  15 us (1%)
    psum x2, waiting for transfers between devices, on_device(): probe_total = lax.psum(probe_term, ('ty', 'tx'))  252 us
    another operation x2, loops' own time, accumulate(): lax.fori_loop(0, terms.shape[0], add_slot, jnp.zeros(extended_shape, jnp....  183 us
    gather x144, local copies, waits for them, and re-layouts  160 us
    dynamic_update_slice x48, local copies, waits for them, and re-layouts, add_slot(): lax.dynamic_update_slice(total, present_block + terms[slot_number], corner)  146 us
    dynamic_slice x96, local copies, waits for them, and re-layouts, add_slot(): corner = (anchor, tops[slot_number], lefts[slot_number])  88.6 us
    all_to_all x2, waiting for transfers between devices, on_device(): lax.all_to_all(placed.reshape(band_count, CAP, 2, width, width), 'ty', sp...  71.3 us
    ppermute x8, waiting for transfers between devices, shifted(): lax.ppermute(value, axis, [(source, source + steps) for source in range(l...  58.1 us
    add x48, other arithmetic, add_slot(): present_block + terms[slot_number]  51.9 us
  transfers between devices with their start and end apart: 16, of which 13 were waited for; matrix products, arithmetic and copies ran while one was open for 1% of the time, Pallas kernels for 0%

commit v1 on v0

v1 whole, which is shorter than its diff:
```python
import functools
import math

import jax
import jax.numpy as jnp
import ml_dtypes
import numpy as np
from jax import lax
from jax.experimental import pallas as pl
from jax.experimental.pallas import tpu as pltpu
from jax.sharding import PartitionSpec as P

CAP = 3
STEPS = 2
GROUP = 4
ROWS = 8

OBJECT_RATE = 0.25
PROBE_RATE = 1.0


def shifted(value, axis, steps):
    count = lax.axis_size(axis)
    leading, last = (max(0, -steps), min(count, count - steps))
    return lax.ppermute(value, axis, [(source, source + steps) for source in range(leading, last)])


def sum_everywhere(value, axes):
    for axis in axes:
        count = lax.axis_size(axis)
        step = 1
        while step < count:
            pairs = [(source, source ^ step) for source in range(count)]
            value = value + lax.ppermute(value, axis, pairs)
            step *= 2
    return value


def split_table(table):
    high = table.astype(ml_dtypes.bfloat16)
    low = (table - high.astype(np.float64)).astype(ml_dtypes.bfloat16)
    return high, low


def dft_tables(width):
    counter = np.arange(width)
    radians = (counter[:, None] * counter[None, :] % width) * (2.0 * math.pi / width)
    cos = np.cos(radians) / math.sqrt(width)
    sin = -np.sin(radians) / math.sqrt(width)
    plus = np.block([[cos, -sin], [sin, cos]])
    minus = np.block([[cos, sin], [-sin, cos]])

    def left(table):
        high, low = split_table(table)
        return np.concatenate([high, low, high], axis=1)

    def right(table):
        high, low = split_table(table)
        return np.concatenate([high, low, high], axis=0)

    return left(plus), right(minus), right(plus), left(minus)


def split(value):
    high = value.astype(jnp.bfloat16)
    low = (value - high.astype(jnp.float32)).astype(jnp.bfloat16)
    return high, low


def left_apply(table, parts):
    data = jnp.concatenate(
        [jnp.concatenate([re for re, _ in parts], axis=1), jnp.concatenate([im for _, im in parts], axis=1)],
        axis=0,
    )
    high, low = split(data)
    out = jnp.dot(table, jnp.concatenate([high, high, low], axis=0), preferred_element_type=jnp.float32)
    width = out.shape[0] // 2
    return [
        (out[:width, i * width : (i + 1) * width], out[width:, i * width : (i + 1) * width])
        for i in range(len(parts))
    ]


def right_apply(table, parts):
    data = jnp.concatenate([jnp.concatenate([re, im], axis=1) for re, im in parts], axis=0)
    high, low = split(data)
    out = jnp.dot(jnp.concatenate([high, high, low], axis=1), table, preferred_element_type=jnp.float32)
    width = out.shape[1] // 2
    return [
        (out[i * width : (i + 1) * width, :width], out[i * width : (i + 1) * width, width:])
        for i in range(len(parts))
    ]


def step_kernel(
    tops, lefts, extended, probe, measured, table_a, table_b, table_c, table_d, gradient, probe_gradient
):
    width = probe.shape[1]
    slots = measured.shape[0]
    gradient[...] = jnp.zeros_like(gradient)
    probe_gradient[...] = jnp.zeros_like(probe_gradient)
    tiles = width // ROWS
    lane = lax.broadcasted_iota(jnp.int32, (tiles + 1, ROWS, width), 2)
    row = lax.broadcasted_iota(jnp.int32, (tiles, ROWS, width), 1)

    def corner(slot):
        top = jnp.maximum(tops[slot], 0)
        left = lefts[slot]
        top_base = pl.multiple_of(top // ROWS * ROWS, ROWS)
        left_base = pl.multiple_of(left // width * width, width)
        return top_base, top - top_base, left_base, left - left_base

    def cut(slot):
        top_base, down, left_base, off = corner(slot)
        rows = pl.ds(top_base, width + ROWS)
        out = []
        for part in range(2):
            near = extended[part, rows, pl.ds(left_base, width)].reshape(lane.shape)
            far = extended[part, rows, pl.ds(left_base + width, width)].reshape(lane.shape)
            value = pltpu.roll(jnp.where(lane < off, far, near), lax.rem(width - off, width), 2)
            value = pltpu.roll(value, lax.rem(ROWS - down, ROWS), 1)
            value = jnp.where(row < ROWS - down, value[:tiles], value[1:])
            out.append(value.reshape(width, width))
        return out

    def add(slot, terms):
        top_base, down, left_base, off = corner(slot)
        rows = pl.ds(top_base, width + ROWS)
        for part in range(2):
            value = pltpu.roll(terms[part].reshape(row.shape), down, 1)
            value = pltpu.roll(value, off, 2)
            upper = jnp.where(row >= down, value, 0.0)
            lower = jnp.where(row >= down, 0.0, value)
            edge = jnp.zeros((1, ROWS, width), jnp.float32)
            value = jnp.concatenate([upper, edge], axis=0) + jnp.concatenate([edge, lower], axis=0)
            near = jnp.where(lane < off, 0.0, value).reshape(width + ROWS, width)
            far = jnp.where(lane < off, value, 0.0).reshape(width + ROWS, width)
            gradient[part, rows, pl.ds(left_base, width)] += near
            gradient[part, rows, pl.ds(left_base + width, width)] += far

    def body(group, carry):
        pairs = [
            [group * GROUP + 2 * pair, group * GROUP + 2 * pair + 1] for pair in range(GROUP // 2)
        ]
        for pair in pairs:
            patches = [cut(slot) for slot in pair]
            probe_re, probe_im = probe[0], probe[1]
            waves = [
                (probe_re * re - probe_im * im, probe_re * im + probe_im * re) for re, im in patches
            ]
            far = right_apply(table_b[...], left_apply(table_a[...], waves))
            scaled = []
            for slot, (re, im) in zip(pair, far):
                filled = jnp.where(tops[slot] >= 0, 1.0, 0.0)
                misfit = (re * re + im * im - measured[slot]) * filled
                scaled.append((misfit * re, misfit * im))
            back = left_apply(table_d[...], right_apply(table_c[...], scaled))
            probe_terms = [
                (qr * br + qi * bi, qr * bi - qi * br) for (qr, qi), (br, bi) in zip(patches, back)
            ]
            probe_gradient[0] += probe_terms[0][0] + probe_terms[1][0]
            probe_gradient[1] += probe_terms[0][1] + probe_terms[1][1]
            for slot, (br, bi) in zip(pair, back):
                add(slot, (probe_re * br + probe_im * bi, probe_re * bi - probe_im * br))
        return carry

    lax.fori_loop(0, slots // GROUP, body, 0)


def run_step(tops, lefts, extended, probe, measured, tables):
    vmem = pl.BlockSpec(memory_space=pltpu.VMEM)
    smem = pl.BlockSpec(memory_space=pltpu.SMEM)
    width = probe.shape[1]
    slots = measured.shape[0]
    return pl.pallas_call(
        step_kernel,
        out_shape=(
            jax.ShapeDtypeStruct(extended.shape, jnp.float32),
            jax.ShapeDtypeStruct(probe.shape, jnp.float32),
        ),
        in_specs=[smem, smem] + [vmem] * 7,
        out_specs=(vmem, vmem),
        compiler_params=pltpu.CompilerParams(vmem_limit_bytes=40 * 1024 * 1024),
        cost_estimate=pl.CostEstimate(
            flops=slots * 24 * 8 * width**3, bytes_accessed=8 * 1024 * 1024, transcendentals=0
        ),
    )(tops, lefts, extended, probe, measured, *tables)


def extend_tile(object_field, width):
    right_part = shifted(object_field[:, :, :width], "tx", -1)
    widened = jnp.concatenate([object_field, right_part], axis=2)
    lower_part = shifted(widened[:, :width, :], "ty", -1)
    return jnp.concatenate([widened, lower_part], axis=1)


def sum_extended(total, tile_rows, tile_cols, width):
    from_left = shifted(total[:, :, tile_cols:], "tx", 1)
    from_right = shifted(total[:, :, :width], "tx", -1)
    total = jnp.concatenate(
        [
            total[:, :, :width] + from_left,
            total[:, :, width:tile_cols],
            total[:, :, tile_cols:] + from_right,
        ],
        axis=2,
    )
    from_above = shifted(total[:, tile_rows:, :], "ty", 1)
    from_below = shifted(total[:, :width, :], "ty", -1)
    return jnp.concatenate(
        [
            total[:, :width, :] + from_above,
            total[:, width:tile_rows, :],
            total[:, tile_rows:, :] + from_below,
        ],
        axis=1,
    )


def fold_back(total, tile_rows, tile_cols, width):
    spill_down = shifted(total[:, tile_rows:, :], "ty", 1)
    upper_part = total[:, :tile_rows, :]
    upper_part = jnp.concatenate(
        [upper_part[:, :width, :] + spill_down, upper_part[:, width:, :]], axis=1
    )
    spill_right = shifted(upper_part[:, :, tile_cols:], "tx", 1)
    return jnp.concatenate(
        [upper_part[:, :, :width] + spill_right, upper_part[:, :, width:tile_cols]], axis=2
    )


def on_device(object_field, probe_field, owners, row_offsets, col_offsets, intensities):
    band_count = lax.axis_size("ty")
    strip_count = lax.axis_size("tx")
    tile_rows = object_field.shape[1]
    tile_cols = object_field.shape[2]
    width = probe_field.shape[1]
    batch_rows = row_offsets.shape[1]
    slot_count = band_count * CAP
    strip_index = lax.axis_index("tx")
    tables = [jnp.asarray(table) for table in dft_tables(width)]
    probe_scale = PROBE_RATE / (batch_rows * band_count * strip_count)

    owner_rows = owners[:, :, 0]
    position_ids = jnp.arange(batch_rows, dtype=jnp.int32)
    earlier = (owner_rows[:, None, :] == owner_rows[:, :, None]) & (
        position_ids[None, None, :] < position_ids[None, :, None]
    )
    slot_of = owner_rows * CAP + jnp.sum(earlier.astype(jnp.int32), axis=2)
    top_local = (
        jnp.minimum(owner_rows * tile_rows + row_offsets, tile_rows * band_count - width)
        - owner_rows * tile_rows
    )
    left_local = (
        jnp.minimum(strip_index * tile_cols + col_offsets, tile_cols * strip_count - width)
        - strip_index * tile_cols
    )
    slot_ids = jnp.arange(slot_count, dtype=jnp.int32)
    matches = slot_of[:, None, :] == slot_ids[None, :, None]
    filled = jnp.any(matches, axis=2)

    def by_slot(values):
        return jnp.sum(jnp.where(matches, values[:, None, :], 0), axis=2)

    want_top = jnp.where(filled, by_slot(top_local), -1)
    want_left = by_slot(left_local)
    holder = by_slot(jnp.broadcast_to(position_ids[None], slot_of.shape))
    wanted = jnp.stack([want_top, want_left]).reshape(2 * STEPS, band_count, CAP)
    received = lax.all_to_all(wanted, "ty", split_axis=1, concat_axis=1, tiled=True).reshape(
        2, STEPS, slot_count
    )

    def exchange(step_number):
        chosen = jnp.take(intensities[step_number], holder[step_number], axis=0, mode="clip")
        moved = lax.all_to_all(
            chosen.reshape(band_count, CAP, width, width), "ty", split_axis=0, concat_axis=0, tiled=True
        )
        return moved.reshape(slot_count, width, width)

    measured = [exchange(step_number) for step_number in range(STEPS)]
    extended = extend_tile(object_field, width)
    for step_number in range(STEPS):
        gathered, probe_term = run_step(
            received[0, step_number],
            received[1, step_number],
            extended,
            probe_field,
            measured[step_number],
            tables,
        )
        probe_total = sum_everywhere(probe_term, ("ty", "tx"))
        if step_number < STEPS - 1:
            extended = extended - OBJECT_RATE * sum_extended(gathered, tile_rows, tile_cols, width)
        else:
            object_field = extended[:, :tile_rows, :tile_cols] - OBJECT_RATE * fold_back(
                gathered, tile_rows, tile_cols, width
            )
        probe_field = probe_field - probe_scale * probe_total
    return (object_field, probe_field)


def solution(mesh):
    in_specs = (
        P(None, "ty", "tx"),
        P(),
        P(None, ("ty", "tx"), None),
        P(None, ("ty", "tx")),
        P(None, ("ty", "tx")),
        P(None, ("ty", "tx"), None, None),
    )
    out_specs = (P(None, "ty", "tx"), P())
    return jax.shard_map(
        on_device, mesh=mesh, in_specs=in_specs, out_specs=out_specs, check_vma=False
    )
```

time: 1300 us -> 216 us (0.17)
  local copies, waits for them, and re-layouts: 447 us -> 20.8 us
  waiting for transfers between devices: 418 us -> 104 us
  loops' own time: 184 us -> 0 us
  matrix products: 96.8 us -> 0 us
  other arithmetic: 76.8 us -> 12.7 us
  Pallas kernels: 0 us -> 32.2 us
  between operations: 15 us -> 1.11 us
    psum x2 -> x0, waiting for transfers between devices: 252 us -> none  [on_device(): probe_total = lax.psum(probe_term, ('ty', 'tx'))]
    another operation x4 -> x0, loops' own time: 184 us -> none  [the longest x2 183 us: accumulate(): lax.fori_loop(0, terms.shape[0], add_slot, jnp.zeros(extended_shape, jnp....]
    gather x146 -> x2, local copies, waits for them, and re-layouts: 167 us -> 4.99 us  [exchange(): jnp.take(intensities[step_number], holder[step_number], axis=0, mode='clip')]
    dynamic_update_slice x48 -> x0, local copies, waits for them, and re-layouts: 146 us -> none  [add_slot(): lax.dynamic_update_slice(total, present_block + terms[slot_number], corner)]
    all_to_all x4 -> x2, waiting for transfers between devices: 106 us -> 0.01 us  [exchange(): lax.all_to_all(chosen.reshape(band_count, CAP, width, width), 'ty', split...]
    dot_general x32 -> x0, matrix products: 96.8 us -> none  [the longest x16 48.5 us: product_of(): return jnp.einsum('bkn,nm->bkm', data, table, precision=HIGHEST)]
    dynamic_slice x96 -> x0, local copies, waits for them, and re-layouts: 88.6 us -> none  [add_slot(): corner = (anchor, tops[slot_number], lefts[slot_number])]
    ppermute x0 -> x10, waiting for transfers between devices: none -> 66.5 us  [sum_everywhere(): value = value + lax.ppermute(value, axis, pairs)]
  transfers between devices with their start and end apart: 16 -> 21, of which waited for: 13 -> 13; matrix products, arithmetic and copies ran while one was open for 1% -> 9% of each run, Pallas kernels for 0% -> 0%
where the time goes in v1:
time: 216 us; the launch traced here: 215 us
  waiting for transfers between devices  104 us (48%)
  starting transfers between devices  43.9 us (20%)
  Pallas kernels  32.2 us (15%)
  local copies, waits for them, and re-layouts  20.8 us (10%)
  other arithmetic  12.7 us (6%)
    ppermute x10, waiting for transfers between devices, sum_everywhere(): value = value + lax.ppermute(value, axis, pairs)  66.5 us
    ppermute x8, waiting for transfers between devices, shifted(): lax.ppermute(value, axis, [(source, source + steps) for source in range(l...  37.8 us
    pallas_call x2, Pallas kernels, run_step(): pl.pallas_call(step_kernel, out_shape=(jax.ShapeDtypeStruct(extended.shap...  32.2 us
    ppermute x8, starting transfers between devices, shifted(): lax.ppermute(value, axis, [(source, source + steps) for source in range(l...  19.1 us
    ppermute x10, starting transfers between devices, sum_everywhere(): value = value + lax.ppermute(value, axis, pairs)  11.1 us
    unnamed x39, local copies, waits for them, and re-layouts  9.65 us
    all_to_all x2, starting transfers between devices, exchange(): lax.all_to_all(chosen.reshape(band_count, CAP, width, width), 'ty', split...  9.1 us
    gather x2, local copies, waits for them, and re-layouts, exchange(): jnp.take(intensities[step_number], holder[step_number], axis=0, mode='clip')  4.99 us
  transfers between devices with their start and end apart: 21, of which 13 were waited for; matrix products, arithmetic and copies ran while one was open for 9% of the time, Pallas kernels for 0%

profile of v1, /device:TPU:3, one launch (start us, length us, event | category | flops | bytes accessed | tf_op | source)
XLA Modules:
  0.0 215.1 jit_solution(6744627328760498289)
XLA Ops:
  3.3 4.6 %all-to-all-start = ((s32[4,8,3]{2,0,1:T(4,128)}), s32[4,8,3]{2,0,1:T(4,128)S(1)}, u32[]{:S(2)}, u32[]{:S(2)}) async-start(s32[4,8,3]{2,0,1:T(4,128)} %copy.14), calls=%async_computation | async-start | bytes 32768 | tf_op jit(solution)/shard_map/all_to_all | solution.py:269
  10.3 3.3 %slice_bitcast_fusion = (f32[24,128,128]{2,1,0:T(8,128)}, f32[24,128,128]{2,1,0:T(8,128)S(1)}) fusion(f32[2,24,128,128]{3,2,1,0:T(8,128)} %param.15), kind=kLoop, calls=%fused_computation.17 | loop fusion | bytes 6291456 | tf_op jit(solution)/shard_map/squeeze | solution.py:274
  15.9 4.4 %all-to-all-start.1 = ((f32[8,3,128,128]{3,2,1,0:T(8,128)}), f32[8,3,128,128]{3,2,1,0:T(8,128)}, u32[]{:S(2)}, u32[]{:S(2)}) async-start(f32[8,3,128,128]{3,2,1,0:T(8,128)} %bitcast.7), calls=%async_computation.1 | async-start | bytes 3145728 | tf_op jit(solution)/shard_map/all_to_all | solution.py:275
  20.5 3.6 %collective-permute-done = f32[2,512,128]{2,1,0:T(8,128)S(1)} collective-permute-done((f32[2,512,128]{2,1,0:T(8,128)S(1)}, f32[2,512,128]{2,1,0:T(8,128)S(1)}, u32[]{:S(2)}, u32[]{:S(2)}) %collective-permute-start) | collective-permute-done | bytes 524320 | tf_op jit(solution)/shard_map/ppermute | solution.py:25
  25.7 3.0 %collective-permute-start.1 = (f32[2,128,640]{2,1,0:T(8,128)S(1)}, f32[2,128,640]{2,1,0:T(8,128)}, u32[]{:S(2)}, u32[]{:S(2)}) collective-permute-start(f32[2,128,640]{2,1,0:T(8,128)S(1)} %slice.103), channel_id=1, source_target_pairs={{4,0},{8,4},{12,8},{16,12},{20,16},{24,20},{28,24},{5,1},{9,5},{13... | collective-permute-start | bytes 1966088 | tf_op jit(solution)/shard_map/ppermute | solution.py:25
  28.8 17.9 %collective-permute-done.1 = f32[2,128,640]{2,1,0:T(8,128)} collective-permute-done((f32[2,128,640]{2,1,0:T(8,128)S(1)}, f32[2,128,640]{2,1,0:T(8,128)}, u32[]{:S(2)}, u32[]{:S(2)}) %collective-permute-start.1) | collective-permute-done | bytes 655392 | tf_op jit(solution)/shard_map/ppermute | solution.py:25
  52.9 16.1 %shard_map.113 = (f32[2,640,640]{2,1,0:T(8,128)S(1)}, f32[2,128,128]{2,1,0:T(8,128)S(1)}) custom-call(s32[24]{0:T(128)S(1)} %get-tuple-element.24.tops, s32[24]{0:T(128)S(1)} %get-tuple-element.21.lefts, f32[2,640,640]{2,1,0:T(8,128)S(1)} %pad_maximum_fusion.extended, f32[2,128,128]{2,1,0:T(8,128)S(1)} %copy-done, f32[24,128,128]{2,1,0:T(8,128)} %bitcast.8.measured, ...), custom_call_target="tpu_custom_call" | custom-call | flops 9663676416 | bytes 8388608 | tf_op jit(solution)/shard_map/pallas_call | solution.py:175
  69.1 4.3 %collective-permute-start.2 = (f32[2,640,128]{2,1,0:T(8,128)S(1)}, f32[2,640,128]{2,1,0:T(8,128)S(1)}, u32[]{:S(2)}, u32[]{:S(2)}) collective-permute-start(f32[2,640,128]{2,1,0:T(8,128)S(1)} %get-tuple-element.17), channel_id=1, source_target_pairs={{0,1},{1,2},{2,3},{4,5},{5,6},{6,7},{8,9},{9,10},{10,11},{12,13},{... | collective-permute-start | bytes 1966088 | tf_op jit(solution)/shard_map/ppermute | solution.py:25
  74.8 12.1 %collective-permute-done.2 = f32[2,640,128]{2,1,0:T(8,128)S(1)} collective-permute-done((f32[2,640,128]{2,1,0:T(8,128)S(1)}, f32[2,640,128]{2,1,0:T(8,128)S(1)}, u32[]{:S(2)}, u32[]{:S(2)}) %collective-permute-start.2) | collective-permute-done | bytes 655392 | tf_op jit(solution)/shard_map/ppermute | solution.py:25
  87.0 4.1 %collective-permute-done.3 = f32[2,640,128]{2,1,0:T(8,128)S(1)} collective-permute-done((f32[2,640,128]{2,1,0:T(8,128)S(1)}, f32[2,640,128]{2,1,0:T(8,128)S(1)}, u32[]{:S(2)}, u32[]{:S(2)}) %collective-permute-start.3) | collective-permute-done | bytes 655392 | tf_op jit(solution)/shard_map/ppermute | solution.py:25
  92.3 3.2 %collective-permute-start.4 = (f32[2,128,640]{2,1,0:T(8,128)}, f32[2,128,640]{2,1,0:T(8,128)}, u32[]{:S(2)}, u32[]{:S(2)}) collective-permute-start(f32[2,128,640]{2,1,0:T(8,128)} %pad_maximum_fusion.1), channel_id=1, source_target_pairs={{0,4},{4,8},{8,12},{12,16},{16,20},{20,24},{24,28},{1,5},{5,9},{9,... | collective-permute-start | bytes 1966088 | tf_op jit(solution)/shard_map/ppermute | solution.py:25
  95.6 3.2 %gather_fusion.1 = f32[24,128,128]{2,1,0:T(8,128)} fusion(f32[24,128,128]{2,1,0:T(8,128)} %get-tuple-element.19, s32[1024]{0:T(1024)S(1)} %pad_clamp_fusion), kind=kCustom, calls=%fused_computation.1 | custom fusion | bytes 3145824 | tf_op jit(solution)/shard_map/jit(_take)/gather | solution.py:274
  98.8 4.7 %all-to-all-start.2 = ((f32[8,3,128,128]{3,2,1,0:T(8,128)}), f32[8,3,128,128]{3,2,1,0:T(8,128)}, u32[]{:S(2)}, u32[]{:S(2)}) async-start(f32[8,3,128,128]{3,2,1,0:T(8,128)} %bitcast.24), calls=%async_computation.2 | async-start | bytes 3145728 | tf_op jit(solution)/shard_map/all_to_all | solution.py:275
  106.0 2.6 %collective-permute-start.5 = (f32[2,128,640]{2,1,0:T(8,128)S(1)}, f32[2,128,640]{2,1,0:T(8,128)S(1)}, u32[]{:S(2)}, u32[]{:S(2)}) collective-permute-start(f32[2,128,640]{2,1,0:T(8,128)S(1)} %get-tuple-element.14), channel_id=1, source_target_pairs={{4,0},{8,4},{12,8},{16,12},{20,16},{24,20},{28,24},{5,1},{9,5},{13... | collective-permute-start | bytes 1966088 | tf_op jit(solution)/shard_map/ppermute | solution.py:25
  108.6 16.0 %collective-permute-done.7 = f32[2,128,128]{2,1,0:T(8,128)S(1)} collective-permute-done((f32[2,128,128]{2,1,0:T(8,128)S(1)}, f32[2,128,128]{2,1,0:T(8,128)S(1)}, u32[]{:S(2)}, u32[]{:S(2)}) %collective-permute-start.7) | collective-permute-done | bytes 131104 | tf_op jit(solution)/shard_map/ppermute | solution.py:34
  125.8 9.8 %collective-permute-done.8 = f32[2,128,128]{2,1,0:T(8,128)S(1)} collective-permute-done((f32[2,128,128]{2,1,0:T(8,128)S(1)}, f32[2,128,128]{2,1,0:T(8,128)S(1)}, u32[]{:S(2)}, u32[]{:S(2)}) %collective-permute-start.8) | collective-permute-done | bytes 131104 | tf_op jit(solution)/shard_map/ppermute | solution.py:34
  137.0 3.3 %collective-permute-done.9 = f32[2,128,128]{2,1,0:T(8,128)S(1)} collective-permute-done((f32[2,128,128]{2,1,0:T(8,128)S(1)}, f32[2,128,128]{2,1,0:T(8,128)S(1)}, u32[]{:S(2)}, u32[]{:S(2)}) %collective-permute-start.9) | collective-permute-done | bytes 131104 | tf_op jit(solution)/shard_map/ppermute | solution.py:34
  140.3 2.4 %collective-permute-start.10 = (f32[2,128,128]{2,1,0:T(8,128)S(1)}, f32[2,128,128]{2,1,0:T(8,128)S(1)}, u32[]{:S(2)}, u32[]{:S(2)}) collective-permute-start(f32[2,128,128]{2,1,0:T(8,128)S(1)} %add.75), channel_id=1, source_target_pairs={{0,2},{1,3},{2,0},{3,1},{4,6},{5,7},{6,4},{7,5},{8,10},{9,11},{10,... | collective-permute-start | bytes 393224 | tf_op jit(solution)/shard_map/ppermute | solution.py:34
  142.7 5.8 %collective-permute-done.10 = f32[2,128,128]{2,1,0:T(8,128)S(1)} collective-permute-done((f32[2,128,128]{2,1,0:T(8,128)S(1)}, f32[2,128,128]{2,1,0:T(8,128)S(1)}, u32[]{:S(2)}, u32[]{:S(2)}) %collective-permute-start.10) | collective-permute-done | bytes 131104 | tf_op jit(solution)/shard_map/ppermute | solution.py:34
  155.1 16.1 %shard_map.114 = (f32[2,640,640]{2,1,0:T(8,128)S(1)}, f32[2,128,128]{2,1,0:T(8,128)S(1)}) custom-call(s32[24]{0:T(128)S(1)} %get-tuple-element.23.tops, s32[24]{0:T(128)S(1)} %get-tuple-element.22.lefts, f32[2,640,640]{2,1,0:T(8,128)S(1)} %fusion.3.extended, f32[2,128,128]{2,1,0:T(8,128)S(1)} %multiply_subtract_fusion.1.probe, ...), custom_call_target="tpu_custom_call" | custom-call | flops 9663676416 | bytes 8388608 | tf_op jit(solution)/shard_map/pallas_call | solution.py:175
  177.7 9.4 %collective-permute-done.14 = f32[2,128,128]{2,1,0:T(8,128)S(1)} collective-permute-done((f32[2,128,128]{2,1,0:T(8,128)S(1)}, f32[2,128,128]{2,1,0:T(8,128)S(1)}, u32[]{:S(2)}, u32[]{:S(2)}) %collective-permute-start.14) | collective-permute-done | bytes 131104 | tf_op jit(solution)/shard_map/ppermute | solution.py:34
  191.1 11.5 %collective-permute-done.16 = f32[2,128,128]{2,1,0:T(8,128)S(1)} collective-permute-done((f32[2,128,128]{2,1,0:T(8,128)S(1)}, f32[2,128,128]{2,1,0:T(8,128)S(1)}, u32[]{:S(2)}, u32[]{:S(2)}) %collective-permute-start.16) | collective-permute-done | bytes 131104 | tf_op jit(solution)/shard_map/ppermute | solution.py:34
  202.7 3.2 %collective-permute-start.17 = (f32[2,128,128]{2,1,0:T(8,128)S(1)}, f32[2,128,128]{2,1,0:T(8,128)S(1)}, u32[]{:S(2)}, u32[]{:S(2)}) collective-permute-start(f32[2,128,128]{2,1,0:T(8,128)S(1)} %add.82), channel_id=1, source_target_pairs={{0,2},{1,3},{2,0},{3,1},{4,6},{5,7},{6,4},{7,5},{8,10},{9,11},{10,... | collective-permute-start | bytes 393224 | tf_op jit(solution)/shard_map/ppermute | solution.py:34
  205.9 6.8 %collective-permute-done.17 = f32[2,128,128]{2,1,0:T(8,128)S(1)} collective-permute-done((f32[2,128,128]{2,1,0:T(8,128)S(1)}, f32[2,128,128]{2,1,0:T(8,128)S(1)}, u32[]{:S(2)}, u32[]{:S(2)}) %collective-permute-start.17) | collective-permute-done | bytes 131104 | tf_op jit(solution)/shard_map/ppermute | solution.py:34
  (104 shorter events, 42.5 us)
Async XLA Ops:
  3.3 12.6 %all-to-all-start = ((s32[4,8,3]{2,0,1:T(4,128)}), s32[4,8,3]{2,0,1:T(4,128)S(1)}, u32[]{:S(2)}, u32[]{:S(2)}) async-start(s32[4,8,3]{2,0,1:T(4,128)} %copy.14), calls=%async_computation | async-start | bytes 32768 | tf_op jit(solution)/shard_map/all_to_all | solution.py:269
  9.0 15.1 %collective-permute-start = (f32[2,512,128]{2,1,0:T(8,128)S(1)}, f32[2,512,128]{2,1,0:T(8,128)S(1)}, u32[]{:S(2)}, u32[]{:S(2)}) collective-permute-start(f32[2,512,128]{2,1,0:T(8,128)S(1)} %slice.76), channel_id=1, source_target_pairs={{1,0},{2,1},{3,2},{5,4},{6,5},{7,6},{9,8},{10,9},{11,10},{13,12},{... | collective-permute-start | bytes 1572872 | tf_op jit(solution)/shard_map/ppermute | solution.py:25
  15.9 32.9 %all-to-all-start.1 = ((f32[8,3,128,128]{3,2,1,0:T(8,128)}), f32[8,3,128,128]{3,2,1,0:T(8,128)}, u32[]{:S(2)}, u32[]{:S(2)}) async-start(f32[8,3,128,128]{3,2,1,0:T(8,128)} %bitcast.7), calls=%async_computation.1 | async-start | bytes 3145728 | tf_op jit(solution)/shard_map/all_to_all | solution.py:275
  25.7 21.0 %collective-permute-start.1 = (f32[2,128,640]{2,1,0:T(8,128)S(1)}, f32[2,128,640]{2,1,0:T(8,128)}, u32[]{:S(2)}, u32[]{:S(2)}) collective-permute-start(f32[2,128,640]{2,1,0:T(8,128)S(1)} %slice.103), channel_id=1, source_target_pairs={{4,0},{8,4},{12,8},{16,12},{20,16},{24,20},{28,24},{5,1},{9,5},{13... | collective-permute-start | bytes 1966088 | tf_op jit(solution)/shard_map/ppermute | solution.py:25
  69.1 17.9 %collective-permute-start.2 = (f32[2,640,128]{2,1,0:T(8,128)S(1)}, f32[2,640,128]{2,1,0:T(8,128)S(1)}, u32[]{:S(2)}, u32[]{:S(2)}) collective-permute-start(f32[2,640,128]{2,1,0:T(8,128)S(1)} %get-tuple-element.17), channel_id=1, source_target_pairs={{0,1},{1,2},{2,3},{4,5},{5,6},{6,7},{8,9},{9,10},{10,11},{12,13},{... | collective-permute-start | bytes 1966088 | tf_op jit(solution)/shard_map/ppermute | solution.py:25
  73.4 17.7 %collective-permute-start.3 = (f32[2,640,128]{2,1,0:T(8,128)S(1)}, f32[2,640,128]{2,1,0:T(8,128)S(1)}, u32[]{:S(2)}, u32[]{:S(2)}) collective-permute-start(f32[2,640,128]{2,1,0:T(8,128)S(1)} %get-tuple-element.18), channel_id=1, source_target_pairs={{1,0},{2,1},{3,2},{5,4},{6,5},{7,6},{9,8},{10,9},{11,10},{13,12},{... | collective-permute-start | bytes 1966088 | tf_op jit(solution)/shard_map/ppermute | solution.py:25
  92.3 12.3 %collective-permute-start.4 = (f32[2,128,640]{2,1,0:T(8,128)}, f32[2,128,640]{2,1,0:T(8,128)}, u32[]{:S(2)}, u32[]{:S(2)}) collective-permute-start(f32[2,128,640]{2,1,0:T(8,128)} %pad_maximum_fusion.1), channel_id=1, source_target_pairs={{0,4},{4,8},{8,12},{12,16},{16,20},{20,24},{24,28},{1,5},{5,9},{9,... | collective-permute-start | bytes 1966088 | tf_op jit(solution)/shard_map/ppermute | solution.py:25
  95.5 8.0 %collective-permute-start.6 = (f32[2,128,128]{2,1,0:T(8,128)S(1)}, f32[2,128,128]{2,1,0:T(8,128)}, u32[]{:S(2)}, u32[]{:S(2)}) collective-permute-start(f32[2,128,128]{2,1,0:T(8,128)S(1)} %get-tuple-element.7), channel_id=1, source_target_pairs={{0,4},{4,0},{8,12},{12,8},{16,20},{20,16},{24,28},{28,24},{1,5},{5... | collective-permute-start | bytes 393224 | tf_op jit(solution)/shard_map/ppermute | solution.py:34
  98.8 52.3 %all-to-all-start.2 = ((f32[8,3,128,128]{3,2,1,0:T(8,128)}), f32[8,3,128,128]{3,2,1,0:T(8,128)}, u32[]{:S(2)}, u32[]{:S(2)}) async-start(f32[8,3,128,128]{3,2,1,0:T(8,128)} %bitcast.24), calls=%async_computation.2 | async-start | bytes 3145728 | tf_op jit(solution)/shard_map/all_to_all | solution.py:275
  104.5 20.1 %collective-permute-start.7 = (f32[2,128,128]{2,1,0:T(8,128)S(1)}, f32[2,128,128]{2,1,0:T(8,128)S(1)}, u32[]{:S(2)}, u32[]{:S(2)}) collective-permute-start(f32[2,128,128]{2,1,0:T(8,128)S(1)} %add.72), channel_id=1, source_target_pairs={{0,8},{4,12},{8,0},{12,4},{16,24},{20,28},{24,16},{28,20},{1,9},{5... | collective-permute-start | bytes 393224 | tf_op jit(solution)/shard_map/ppermute | solution.py:34
  104.6 45.1 %copy-start.12 = (f32[2,512,640]{2,1,0:T(8,128)S(1)}, f32[2,512,640]{2,1,0:T(8,128)}, u32[]{:S(2)}) copy-start(f32[2,512,640]{2,1,0:T(8,128)} %copy-done.11) | copy-start | bytes 7864324
  106.0 43.7 %copy-start.10 = (f32[2,640,384]{2,1,0:T(8,128)S(1)}, f32[2,640,384]{2,1,0:T(8,128)}, u32[]{:S(2)}) copy-start(f32[2,640,384]{2,1,0:T(8,128)} %copy-done.9) | copy-start | bytes 5898244
  106.0 43.7 %copy-start.14 = (f32[2,640,128]{2,1,0:T(8,128)S(1)}, f32[2,640,128]{2,1,0:T(8,128)}, u32[]{:S(2)}) copy-start(f32[2,640,128]{2,1,0:T(8,128)} %copy-done.13) | copy-start | bytes 1966084
  106.0 42.5 %collective-permute-start.5 = (f32[2,128,640]{2,1,0:T(8,128)S(1)}, f32[2,128,640]{2,1,0:T(8,128)S(1)}, u32[]{:S(2)}, u32[]{:S(2)}) collective-permute-start(f32[2,128,640]{2,1,0:T(8,128)S(1)} %get-tuple-element.14), channel_id=1, source_target_pairs={{4,0},{8,4},{12,8},{16,12},{20,16},{24,20},{28,24},{5,1},{9,5},{13... | collective-permute-start | bytes 1966088 | tf_op jit(solution)/shard_map/ppermute | solution.py:25
  124.6 11.1 %collective-permute-start.8 = (f32[2,128,128]{2,1,0:T(8,128)S(1)}, f32[2,128,128]{2,1,0:T(8,128)S(1)}, u32[]{:S(2)}, u32[]{:S(2)}) collective-permute-start(f32[2,128,128]{2,1,0:T(8,128)S(1)} %add.73), channel_id=1, source_target_pairs={{0,16},{4,20},{8,24},{12,28},{16,0},{20,4},{24,8},{28,12},{1,17},{... | collective-permute-start | bytes 393224 | tf_op jit(solution)/shard_map/ppermute | solution.py:34
  135.7 4.6 %collective-permute-start.9 = (f32[2,128,128]{2,1,0:T(8,128)S(1)}, f32[2,128,128]{2,1,0:T(8,128)S(1)}, u32[]{:S(2)}, u32[]{:S(2)}) collective-permute-start(f32[2,128,128]{2,1,0:T(8,128)S(1)} %add.74), channel_id=1, source_target_pairs={{0,1},{1,0},{2,3},{3,2},{4,5},{5,4},{6,7},{7,6},{8,9},{9,8},{10,11... | collective-permute-start | bytes 393224 | tf_op jit(solution)/shard_map/ppermute | solution.py:34
  140.3 8.1 %collective-permute-start.10 = (f32[2,128,128]{2,1,0:T(8,128)S(1)}, f32[2,128,128]{2,1,0:T(8,128)S(1)}, u32[]{:S(2)}, u32[]{:S(2)}) collective-permute-start(f32[2,128,128]{2,1,0:T(8,128)S(1)} %add.75), channel_id=1, source_target_pairs={{0,2},{1,3},{2,0},{3,1},{4,6},{5,7},{6,4},{7,5},{8,10},{9,11},{10,... | collective-permute-start | bytes 393224 | tf_op jit(solution)/shard_map/ppermute | solution.py:34
  171.3 16.0 %collective-permute-start.11 = (f32[2,128,640]{2,1,0:T(8,128)S(1)}, f32[2,128,640]{2,1,0:T(8,128)S(1)}, u32[]{:S(2)}, u32[]{:S(2)}) collective-permute-start(f32[2,128,640]{2,1,0:T(8,128)S(1)} %slice.94), channel_id=1, source_target_pairs={{0,4},{4,8},{8,12},{12,16},{16,20},{20,24},{24,28},{1,5},{5,9},{9,... | collective-permute-start | bytes 1966088 | tf_op jit(solution)/shard_map/ppermute | solution.py:25
  173.2 3.3 %collective-permute-start.13 = (f32[2,128,128]{2,1,0:T(8,128)S(1)}, f32[2,128,128]{2,1,0:T(8,128)S(1)}, u32[]{:S(2)}, u32[]{:S(2)}) collective-permute-start(f32[2,128,128]{2,1,0:T(8,128)S(1)} %get-tuple-element.9), channel_id=1, source_target_pairs={{0,4},{4,0},{8,12},{12,8},{16,20},{20,16},{24,28},{28,24},{1,5},{5... | collective-permute-start | bytes 393224 | tf_op jit(solution)/shard_map/ppermute | solution.py:34
  176.5 10.6 %collective-permute-start.14 = (f32[2,128,128]{2,1,0:T(8,128)S(1)}, f32[2,128,128]{2,1,0:T(8,128)S(1)}, u32[]{:S(2)}, u32[]{:S(2)}) collective-permute-start(f32[2,128,128]{2,1,0:T(8,128)S(1)} %add.79), channel_id=1, source_target_pairs={{0,8},{4,12},{8,0},{12,4},{16,24},{20,28},{24,16},{28,20},{1,9},{5... | collective-permute-start | bytes 393224 | tf_op jit(solution)/shard_map/ppermute | solution.py:34
  187.1 3.9 %collective-permute-start.15 = (f32[2,128,128]{2,1,0:T(8,128)S(1)}, f32[2,128,128]{2,1,0:T(8,128)S(1)}, u32[]{:S(2)}, u32[]{:S(2)}) collective-permute-start(f32[2,128,128]{2,1,0:T(8,128)S(1)} %add.80), channel_id=1, source_target_pairs={{0,16},{4,20},{8,24},{12,28},{16,0},{20,4},{24,8},{28,12},{1,17},{... | collective-permute-start | bytes 393224 | tf_op jit(solution)/shard_map/ppermute | solution.py:34
  187.4 26.0 %collective-permute-start.12 = (f32[2,512,128]{2,1,0:T(8,128)S(1)}, f32[2,512,128]{2,1,0:T(8,128)S(1)}, u32[]{:S(2)}, u32[]{:S(2)}) collective-permute-start(f32[2,512,128]{2,1,0:T(8,128)S(1)} %pad_maximum_fusion.3), channel_id=1, source_target_pairs={{0,1},{1,2},{2,3},{4,5},{5,6},{6,7},{8,9},{9,10},{10,11},{12,13},{... | collective-permute-start | bytes 1572872 | tf_op jit(solution)/shard_map/ppermute | solution.py:25
  191.0 11.6 %collective-permute-start.16 = (f32[2,128,128]{2,1,0:T(8,128)S(1)}, f32[2,128,128]{2,1,0:T(8,128)S(1)}, u32[]{:S(2)}, u32[]{:S(2)}) collective-permute-start(f32[2,128,128]{2,1,0:T(8,128)S(1)} %add.81), channel_id=1, source_target_pairs={{0,1},{1,0},{2,3},{3,2},{4,5},{5,4},{6,7},{7,6},{8,9},{9,8},{10,11... | collective-permute-start | bytes 393224 | tf_op jit(solution)/shard_map/ppermute | solution.py:34
  202.7 9.9 %collective-permute-start.17 = (f32[2,128,128]{2,1,0:T(8,128)S(1)}, f32[2,128,128]{2,1,0:T(8,128)S(1)}, u32[]{:S(2)}, u32[]{:S(2)}) collective-permute-start(f32[2,128,128]{2,1,0:T(8,128)S(1)} %add.82), channel_id=1, source_target_pairs={{0,2},{1,3},{2,0},{3,1},{4,6},{5,7},{6,4},{7,5},{8,10},{9,11},{10,... | collective-permute-start | bytes 393224 | tf_op jit(solution)/shard_map/ppermute | solution.py:34
  (16 other events, 138.4 us)

commit v2 on v1

--- a/solution.py
+++ b/solution.py
@@ -19,23 +19,6 @@
 PROBE_RATE = 1.0
 
 
-def shifted(value, axis, steps):
-    count = lax.axis_size(axis)
-    leading, last = (max(0, -steps), min(count, count - steps))
-    return lax.ppermute(value, axis, [(source, source + steps) for source in range(leading, last)])
-
-
-def sum_everywhere(value, axes):
-    for axis in axes:
-        count = lax.axis_size(axis)
-        step = 1
-        while step < count:
-            pairs = [(source, source ^ step) for source in range(count)]
-            value = value + lax.ppermute(value, axis, pairs)
-            step *= 2
-    return value
-
-
 def split_table(table):
     high = table.astype(ml_dtypes.bfloat16)
     low = (table - high.astype(np.float64)).astype(ml_dtypes.bfloat16)
@@ -58,7 +41,7 @@
         high, low = split_table(table)
         return np.concatenate([high, low, high], axis=0)
 
-    return left(plus), right(minus), right(plus), left(minus)
+    return np.stack([left(plus), left(minus)]), np.stack([right(minus), right(plus)])
 
 
 def split(value):
@@ -93,7 +76,7 @@
 
 
 def step_kernel(
-    tops, lefts, extended, probe, measured, table_a, table_b, table_c, table_d, gradient, probe_gradient
+    tops, lefts, extended, probe, measured, left_tables, right_tables, gradient, probe_gradient
 ):
     width = probe.shape[1]
     slots = measured.shape[0]
@@ -148,13 +131,13 @@
             waves = [
                 (probe_re * re - probe_im * im, probe_re * im + probe_im * re) for re, im in patches
             ]
-            far = right_apply(table_b[...], left_apply(table_a[...], waves))
+            far = right_apply(right_tables[0], left_apply(left_tables[0], waves))
             scaled = []
             for slot, (re, im) in zip(pair, far):
                 filled = jnp.where(tops[slot] >= 0, 1.0, 0.0)
                 misfit = (re * re + im * im - measured[slot]) * filled
                 scaled.append((misfit * re, misfit * im))
-            back = left_apply(table_d[...], right_apply(table_c[...], scaled))
+            back = left_apply(left_tables[1], right_apply(right_tables[1], scaled))
             probe_terms = [
                 (qr * br + qi * bi, qr * bi - qi * br) for (qr, qi), (br, bi) in zip(patches, back)
             ]
@@ -178,7 +161,7 @@
             jax.ShapeDtypeStruct(extended.shape, jnp.float32),
             jax.ShapeDtypeStruct(probe.shape, jnp.float32),
         ),
-        in_specs=[smem, smem] + [vmem] * 7,
+        in_specs=[smem, smem] + [vmem] * 5,
         out_specs=(vmem, vmem),
         compiler_params=pltpu.CompilerParams(vmem_limit_bytes=40 * 1024 * 1024),
         cost_estimate=pl.CostEstimate(
@@ -187,45 +170,338 @@
     )(tops, lefts, extended, probe, measured, *tables)
 
 
-def extend_tile(object_field, width):
-    right_part = shifted(object_field[:, :, :width], "tx", -1)
-    widened = jnp.concatenate([object_field, right_part], axis=2)
-    lower_part = shifted(widened[:, :width, :], "ty", -1)
-    return jnp.concatenate([widened, lower_part], axis=1)
-
-
-def sum_extended(total, tile_rows, tile_cols, width):
-    from_left = shifted(total[:, :, tile_cols:], "tx", 1)
-    from_right = shifted(total[:, :, :width], "tx", -1)
-    total = jnp.concatenate(
+def remote(source, target, send, receive, ty, tx):
+    return pltpu.make_async_remote_copy(
+        src_ref=source,
+        dst_ref=target,
+        send_sem=send,
+        recv_sem=receive,
+        device_id=(ty, tx),
+        device_id_type=pl.DeviceIdType.MESH,
+    )
+
+
+def only(condition):
+    return pl.when(condition)
+
+
+def greet(partners):
+    barrier = pltpu.get_barrier_semaphore()
+    count = 0
+    for exists, ty, tx in partners:
+
+        def signal(ty=ty, tx=tx):
+            pl.semaphore_signal(
+                barrier, inc=1, device_id=(ty, tx), device_id_type=pl.DeviceIdType.MESH
+            )
+
+        if exists is True:
+            signal()
+            count = count + 1
+        else:
+            only(exists)(signal)
+            count = count + exists.astype(jnp.int32)
+    pl.semaphore_wait(barrier, count)
+
+
+def peers(band_count, ty, tx):
+    return [(True, lax.rem(ty + k, band_count), tx) for k in range(1, band_count)]
+
+
+def stage_measured(step_number, intensities, holder, staged, outgoing, measured, load_sem, ty):
+    load = pltpu.make_async_copy(intensities.at[step_number], staged, load_sem)
+    load.start()
+    load.wait()
+
+    def place(slot, carry):
+        outgoing[slot] = staged[holder[step_number, slot]]
+        return carry
+
+    lax.fori_loop(0, outgoing.shape[0], place, 0)
+    for own in range(CAP):
+        measured[ty * CAP + own] = staged[holder[step_number, ty * CAP + own]]
+
+
+def measured_copies(band_count, outgoing, measured, send_sems, recv_sems, ty, tx):
+    copies = []
+    for k in range(1, band_count):
+        peer = lax.rem(ty + k, band_count)
+        copies.append(
+            remote(
+                outgoing.at[pl.ds(peer * CAP, CAP)],
+                measured.at[pl.ds(ty * CAP, CAP)],
+                send_sems.at[k - 1],
+                recv_sems.at[k - 1],
+                peer,
+                tx,
+            )
+        )
+    return copies
+
+
+def begin_kernel(
+    sizes, holder, intensities, object_field, wants, measured, extended, received,
+    staged, outgoing, load_sem, own_sem, send_sems, recv_sems, want_send, want_recv, halo_send, halo_recv,
+):
+    band_count, strip_count, width = sizes
+    ty, tx = lax.axis_index("ty"), lax.axis_index("tx")
+    rows, cols = object_field.shape[1:]
+    above, left = ty > 0, tx > 0
+    below, right = ty < band_count - 1, tx < strip_count - 1
+    own = pltpu.make_async_copy(object_field, extended.at[:, :rows, :cols], own_sem)
+    own.start()
+    greet(
+        peers(band_count, ty, tx)
+        + [
+            (left, ty, tx - 1),
+            (right, ty, tx + 1),
+            (above & left, ty - 1, tx - 1),
+            (below & right, ty + 1, tx + 1),
+        ]
+    )
+    want_copies = []
+    for k in range(1, band_count):
+        peer = lax.rem(ty + k, band_count)
+        want_copies.append(
+            remote(wants.at[peer], received.at[ty], want_send.at[k - 1], want_recv.at[k - 1], peer, tx)
+        )
+    for copy in want_copies:
+        copy.start()
+    halos = [
+        (
+            left, right,
+            remote(object_field.at[:, :, :width], extended.at[:, :rows, cols:],
+                   halo_send.at[0], halo_recv.at[0], ty, tx - 1),
+        ),
+        (
+            above, below,
+            remote(object_field.at[:, :width, :], extended.at[:, rows:, :cols],
+                   halo_send.at[1], halo_recv.at[1], ty - 1, tx),
+        ),
+        (
+            above & left, below & right,
+            remote(object_field.at[:, :width, :width], extended.at[:, rows:, cols:],
+                   halo_send.at[2], halo_recv.at[2], ty - 1, tx - 1),
+        ),
+    ]
+    for sends, _, copy in halos:
+        only(sends)(copy.start)
+    stage_measured(0, intensities, holder, staged, outgoing, measured, load_sem, ty)
+    copies = measured_copies(band_count, outgoing, measured, send_sems, recv_sems, ty, tx)
+    for copy in copies:
+        copy.start()
+    received[ty] = wants[ty]
+
+    @only(jnp.logical_not(right))
+    def _():
+        extended[:, :rows, cols:] = jnp.zeros((2, rows, width), jnp.float32)
+
+    @only(jnp.logical_not(below))
+    def _():
+        extended[:, rows:, :cols] = jnp.zeros((2, width, cols), jnp.float32)
+
+    @only(jnp.logical_not(below & right))
+    def _():
+        extended[:, rows:, cols:] = jnp.zeros((2, width, width), jnp.float32)
+
+    own.wait()
+    for copy in want_copies:
+        copy.wait()
+    for sends, receives, copy in halos:
+        only(sends)(copy.wait_send)
+        only(receives)(copy.wait_recv)
+    for copy in copies:
+        copy.wait()
+
+
+def butterfly(band_count, strip_count, ty, tx):
+    partners = []
+    step = 1
+    while step < strip_count:
+        partners.append(("tx", step, (ty, tx + step * (1 - 2 * (tx // step % 2)))))
+        step *= 2
+    step = 1
+    while step < band_count:
+        partners.append(("ty", step, (ty + step * (1 - 2 * (ty // step % 2)), tx)))
+        step *= 2
+    return partners
+
+
+def probe_rounds(partners, probe_term, sums, arrived, send_sems, recv_sems):
+    def source(k):
+        return probe_term if k == 0 else sums.at[k - 1]
+
+    copies = [
+        remote(source(k), arrived.at[k], send_sems.at[k], recv_sems.at[k], *partner)
+        for k, (_, _, partner) in enumerate(partners)
+    ]
+
+    def finish(k):
+        copies[k].wait()
+        sums[k] = source(k)[...] + arrived[k]
+
+    return copies, finish
+
+
+def middle_kernel(
+    sizes, scale, holder, intensities, gradient, probe_term, extended, probe, measured, new_extended, new_probe,
+    staged, outgoing, load_sem, send_sems, recv_sems, side, ends, ends_out, side_send, side_recv, end_send, end_recv,
+    sums, arrived, sum_send, sum_recv,
+):
+    band_count, strip_count, width = sizes
+    ty, tx = lax.axis_index("ty"), lax.axis_index("tx")
+    rows, cols = (size - width for size in extended.shape[1:])
+    above, left = ty > 0, tx > 0
+    below, right = ty < band_count - 1, tx < strip_count - 1
+    partners = butterfly(band_count, strip_count, ty, tx)
+    greet(
+        peers(band_count, ty, tx)
+        + [(left, ty, tx - 1), (right, ty, tx + 1)]
+        + [(True, *partner) for axis, step, partner in partners if axis == "tx" and step > 1]
+    )
+    copies, finish = probe_rounds(partners, probe_term, sums, arrived, sum_send, sum_recv)
+    copies[0].start()
+    sides = [
+        (right, left, remote(gradient.at[:, :, cols:], side.at[0], side_send.at[0], side_recv.at[0], ty, tx + 1)),
+        (left, right, remote(gradient.at[:, :, :width], side.at[1], side_send.at[1], side_recv.at[1], ty, tx - 1)),
+    ]
+    for sends, _, copy in sides:
+        only(sends)(copy.start)
+    stage_measured(1, intensities, holder, staged, outgoing, measured, load_sem, ty)
+    measured_sends = measured_copies(band_count, outgoing, measured, send_sems, recv_sems, ty, tx)
+    for copy in measured_sends:
+        copy.start()
+    for number, (_, receives, _) in enumerate(sides):
+
+        @only(jnp.logical_not(receives))
+        def _(number=number):
+            side[number] = jnp.zeros(side.shape[1:], jnp.float32)
+
+    for k in range(len(copies)):
+        finish(k)
+        if k + 1 < len(copies):
+            copies[k + 1].start()
+    new_probe[...] = probe[...] - scale * sums[len(copies) - 1]
+    for sends, receives, copy in sides:
+        only(sends)(copy.wait_send)
+        only(receives)(copy.wait_recv)
+    for number, first in enumerate((rows, 0)):
+        block = pl.ds(first, width)
+        ends_out[number, :, :, :width] = gradient[:, block, :width] + side[0, :, block, :]
+        ends_out[number, :, :, width:cols] = gradient[:, block, width:cols]
+        ends_out[number, :, :, cols:] = gradient[:, block, cols:] + side[1, :, block, :]
+    end_copies = [
+        (below, above, remote(ends_out.at[0], ends.at[0], end_send.at[0], end_recv.at[0], ty + 1, tx)),
+        (above, below, remote(ends_out.at[1], ends.at[1], end_send.at[1], end_recv.at[1], ty - 1, tx)),
+    ]
+    for sends, _, copy in end_copies:
+        only(sends)(copy.start)
+    for number, (_, receives, _) in enumerate(end_copies):
+
+        @only(jnp.logical_not(receives))
+        def _(number=number):
+            ends[number] = jnp.zeros(ends.shape[1:], jnp.float32)
+
+    inner = pl.ds(width, rows - width)
+    new_extended[:, inner, :width] = extended[:, inner, :width] - OBJECT_RATE * (
+        gradient[:, inner, :width] + side[0, :, inner, :]
+    )
+    new_extended[:, inner, width:cols] = (
+        extended[:, inner, width:cols] - OBJECT_RATE * gradient[:, inner, width:cols]
+    )
+    new_extended[:, inner, cols:] = extended[:, inner, cols:] - OBJECT_RATE * (
+        gradient[:, inner, cols:] + side[1, :, inner, :]
+    )
+    for sends, receives, copy in end_copies:
+        only(sends)(copy.wait_send)
+        only(receives)(copy.wait_recv)
+    new_extended[:, :width, :] = extended[:, :width, :] - OBJECT_RATE * (ends_out[1] + ends[0])
+    new_extended[:, rows:, :] = extended[:, rows:, :] - OBJECT_RATE * (ends_out[0] + ends[1])
+    for copy in measured_sends:
+        copy.wait()
+
+
+def end_kernel(
+    sizes, scale, gradient, probe_term, extended, probe, new_object, new_probe,
+    side, end, corner, halo_send, halo_recv, sums, arrived, sum_send, sum_recv,
+):
+    band_count, strip_count, width = sizes
+    ty, tx = lax.axis_index("ty"), lax.axis_index("tx")
+    rows, cols = new_object.shape[1:]
+    above, left = ty > 0, tx > 0
+    below, right = ty < band_count - 1, tx < strip_count - 1
+    partners = butterfly(band_count, strip_count, ty, tx)
+    greet(
         [
-            total[:, :, :width] + from_left,
-            total[:, :, width:tile_cols],
-            total[:, :, tile_cols:] + from_right,
-        ],
-        axis=2,
-    )
-    from_above = shifted(total[:, tile_rows:, :], "ty", 1)
-    from_below = shifted(total[:, :width, :], "ty", -1)
-    return jnp.concatenate(
-        [
-            total[:, :width, :] + from_above,
-            total[:, width:tile_rows, :],
-            total[:, tile_rows:, :] + from_below,
-        ],
-        axis=1,
-    )
-
-
-def fold_back(total, tile_rows, tile_cols, width):
-    spill_down = shifted(total[:, tile_rows:, :], "ty", 1)
-    upper_part = total[:, :tile_rows, :]
-    upper_part = jnp.concatenate(
-        [upper_part[:, :width, :] + spill_down, upper_part[:, width:, :]], axis=1
-    )
-    spill_right = shifted(upper_part[:, :, tile_cols:], "tx", 1)
-    return jnp.concatenate(
-        [upper_part[:, :, :width] + spill_right, upper_part[:, :, width:tile_cols]], axis=2
+            (left, ty, tx - 1),
+            (right, ty, tx + 1),
+            (above, ty - 1, tx),
+            (below, ty + 1, tx),
+            (above & left, ty - 1, tx - 1),
+            (below & right, ty + 1, tx + 1),
+        ]
+        + [(True, *partner) for _, step, partner in partners if step > 1]
+    )
+    copies, finish = probe_rounds(partners, probe_term, sums, arrived, sum_send, sum_recv)
+    copies[0].start()
+    halos = [
+        (right, left, side, remote(gradient.at[:, :rows, cols:], side, halo_send.at[0], halo_recv.at[0], ty, tx + 1)),
+        (below, above, end, remote(gradient.at[:, rows:, :cols], end, halo_send.at[1], halo_recv.at[1], ty + 1, tx)),
+        (
+            below & right, above & left, corner,
+            remote(gradient.at[:, rows:, cols:], corner, halo_send.at[2], halo_recv.at[2], ty + 1, tx + 1),
+        ),
+    ]
+    for sends, _, _, copy in halos:
+        only(sends)(copy.start)
+    for _, receives, target, _ in halos:
+
+        @only(jnp.logical_not(receives))
+        def _(target=target):
+            target[...] = jnp.zeros(target.shape, jnp.float32)
+
+    new_object[:, width:, width:] = (
+        extended[:, width:rows, width:cols] - OBJECT_RATE * gradient[:, width:rows, width:cols]
+    )
+    for k in range(len(copies)):
+        finish(k)
+        if k + 1 < len(copies):
+            copies[k + 1].start()
+    new_probe[...] = probe[...] - scale * sums[len(copies) - 1]
+    for sends, receives, _, copy in halos:
+        only(sends)(copy.wait_send)
+        only(receives)(copy.wait_recv)
+    new_object[:, width:, :width] = extended[:, width:rows, :width] - OBJECT_RATE * (
+        gradient[:, width:rows, :width] + side[:, width:, :]
+    )
+    new_object[:, :width, width:] = extended[:, :width, width:cols] - OBJECT_RATE * (
+        gradient[:, :width, width:cols] + end[:, :, width:]
+    )
+    new_object[:, :width, :width] = extended[:, :width, :width] - OBJECT_RATE * (
+        gradient[:, :width, :width] + side[:, :width, :] + end[:, :, :width] + corner[...]
+    )
+
+
+VMEM = pl.BlockSpec(memory_space=pltpu.VMEM)
+SMEM = pl.BlockSpec(memory_space=pltpu.SMEM)
+HBM = pl.BlockSpec(memory_space=pl.ANY)
+DMA = pltpu.SemaphoreType.DMA
+
+
+def floats(*shape):
+    return jax.ShapeDtypeStruct(shape, jnp.float32)
+
+
+def communicate(kernel, number, in_specs, shapes, scratch):
+    return pl.pallas_call(
+        kernel,
+        out_shape=shapes,
+        in_specs=in_specs,
+        out_specs=tuple(VMEM for _ in shapes),
+        scratch_shapes=scratch,
+        compiler_params=pltpu.CompilerParams(
+            collective_id=number, has_side_effects=True, vmem_limit_bytes=48 * 1024 * 1024
+        ),
     )
 
 
@@ -265,38 +541,65 @@
     want_top = jnp.where(filled, by_slot(top_local), -1)
     want_left = by_slot(left_local)
     holder = by_slot(jnp.broadcast_to(position_ids[None], slot_of.shape))
-    wanted = jnp.stack([want_top, want_left]).reshape(2 * STEPS, band_count, CAP)
-    received = lax.all_to_all(wanted, "ty", split_axis=1, concat_axis=1, tiled=True).reshape(
-        2, STEPS, slot_count
-    )
-
-    def exchange(step_number):
-        chosen = jnp.take(intensities[step_number], holder[step_number], axis=0, mode="clip")
-        moved = lax.all_to_all(
-            chosen.reshape(band_count, CAP, width, width), "ty", split_axis=0, concat_axis=0, tiled=True
-        )
-        return moved.reshape(slot_count, width, width)
-
-    measured = [exchange(step_number) for step_number in range(STEPS)]
-    extended = extend_tile(object_field, width)
-    for step_number in range(STEPS):
-        gathered, probe_term = run_step(
-            received[0, step_number],
-            received[1, step_number],
-            extended,
-            probe_field,
-            measured[step_number],
-            tables,
-        )
-        probe_total = sum_everywhere(probe_term, ("ty", "tx"))
-        if step_number < STEPS - 1:
-            extended = extended - OBJECT_RATE * sum_extended(gathered, tile_rows, tile_cols, width)
-        else:
-            object_field = extended[:, :tile_rows, :tile_cols] - OBJECT_RATE * fold_back(
-                gathered, tile_rows, tile_cols, width
-            )
-        probe_field = probe_field - probe_scale * probe_total
-    return (object_field, probe_field)
+    sizes = (band_count, strip_count, width)
+    wants = jnp.concatenate([want_top, want_left]).reshape(2 * STEPS, band_count, CAP).transpose(1, 0, 2)
+    wants = jnp.pad(wants, ((0, 0), (0, 8 - 2 * STEPS), (0, 128 - CAP)))
+    staging = [
+        pltpu.VMEM((batch_rows, width, width), jnp.float32),
+        pltpu.VMEM((slot_count, width, width), jnp.float32),
+        DMA,
+    ]
+    pair_sems = [DMA((band_count - 1,)), DMA((band_count - 1,))]
+    measured, extended, received = communicate(
+        functools.partial(begin_kernel, sizes),
+        0,
+        [SMEM, HBM, HBM, VMEM],
+        (
+            floats(slot_count, width, width),
+            floats(2, tile_rows + width, tile_cols + width),
+            jax.ShapeDtypeStruct(wants.shape, jnp.int32),
+        ),
+        staging + [DMA] + pair_sems + pair_sems + [DMA((3,)), DMA((3,))],
+    )(holder, intensities, object_field, wants)
+    received = received[:, : 2 * STEPS, :CAP].transpose(1, 0, 2).reshape(2, STEPS, slot_count)
+    rounds = (band_count * strip_count).bit_length() - 1
+    summing = [
+        pltpu.VMEM((rounds, 2, width, width), jnp.float32),
+        pltpu.VMEM((rounds, 2, width, width), jnp.float32),
+        DMA((rounds,)),
+        DMA((rounds,)),
+    ]
+    gradient, probe_term = run_step(received[0, 0], received[1, 0], extended, probe_field, measured, tables)
+    measured, extended, probe_field = communicate(
+        functools.partial(middle_kernel, sizes, probe_scale),
+        1,
+        [SMEM, HBM] + [VMEM] * 4,
+        (floats(*measured.shape), floats(*extended.shape), floats(*probe_field.shape)),
+        staging
+        + pair_sems
+        + [
+            pltpu.VMEM((2, 2, tile_rows + width, width), jnp.float32),
+            pltpu.VMEM((2, 2, width, tile_cols + width), jnp.float32),
+            pltpu.VMEM((2, 2, width, tile_cols + width), jnp.float32),
+        ]
+        + [DMA((2,))] * 4
+        + summing,
+    )(holder, intensities, gradient, probe_term, extended, probe_field)
+    gradient, probe_term = run_step(received[0, 1], received[1, 1], extended, probe_field, measured, tables)
+    return communicate(
+        functools.partial(end_kernel, sizes, probe_scale),
+        2,
+        [VMEM] * 4,
+        (floats(*object_field.shape), floats(*probe_field.shape)),
+        [
+            pltpu.VMEM((2, tile_rows, width), jnp.float32),
+            pltpu.VMEM((2, width, tile_cols), jnp.float32),
+            pltpu.VMEM((2, width, width), jnp.float32),
+            DMA((3,)),
+            DMA((3,)),
+        ]
+        + summing,
+    )(gradient, probe_term, extended, probe_field)
 
 
 def solution(mesh):

time: 216 us -> 164 us (0.76)
  Pallas kernels: 32.2 us -> 150 us
  waiting for transfers between devices: 104 us -> 0 us
  starting transfers between devices: 43.9 us -> 0 us
  local copies, waits for them, and re-layouts: 20.8 us -> 9.4 us
  other arithmetic: 12.7 us -> 1.99 us
    pallas_call x0 -> x3, Pallas kernels: none -> 120 us  [the longest x1 55.5 us: on_device(): communicate(functools.partial(middle_kernel, sizes, probe_scale), 1, [SME...]
    ppermute x18 -> x0, waiting for transfers between devices: 104 us -> none  [the longest x10 66.5 us: sum_everywhere(): value = value + lax.ppermute(value, axis, pairs)]
    ppermute x18 -> x0, starting transfers between devices: 30.2 us -> none  [the longest x8 19.1 us: shifted(): lax.ppermute(value, axis, [(source, source + steps) for source in range(l...]
    all_to_all x3 -> x0, starting transfers between devices: 13.7 us -> none  [the longest x2 9.1 us: exchange(): lax.all_to_all(chosen.reshape(band_count, CAP, width, width), 'ty', split...]
    gather x2 -> x0, local copies, waits for them, and re-layouts: 4.99 us -> none  [exchange(): jnp.take(intensities[step_number], holder[step_number], axis=0, mode='clip')]
    sub x5 -> x0, other arithmetic: 4.47 us -> none  [the longest x1 1.67 us: on_device(): extended[:, :tile_rows, :tile_cols]]
    squeeze x2 -> x1, local copies, waits for them, and re-layouts: 3.34 us -> 0.01 us  [on_device(): received[1, 0]]
    add x13 -> x1, other arithmetic: 3.8 us -> 0.72 us  [on_device(): slot_of = owner_rows * CAP + jnp.sum(earlier.astype(jnp.int32), axis=2)]
  transfers between devices with their start and end apart: 21 -> 0, of which waited for: 13 -> 0; matrix products, arithmetic and copies ran while one was open for 9% -> 0% of each run, Pallas kernels for 0% -> 0%
where the time goes in v2:
time: 164 us; the launch traced here: 162 us
  Pallas kernels  150 us (91%)
  local copies, waits for them, and re-layouts  9.4 us (6%)
  other arithmetic  1.99 us (1%)
    pallas_call x1, Pallas kernels, on_device(): communicate(functools.partial(middle_kernel, sizes, probe_scale), 1, [SME...  55.5 us
    pallas_call x1, Pallas kernels, on_device(): communicate(functools.partial(end_kernel, sizes, probe_scale), 2, [VMEM]...  32.5 us
    pallas_call x1, Pallas kernels, on_device(): communicate(functools.partial(begin_kernel, sizes), 0, [SMEM, HBM, HBM, V...  31.7 us
    pallas_call x2, Pallas kernels, run_step(): pl.pallas_call(step_kernel, out_shape=(jax.ShapeDtypeStruct(extended.shap...  30.5 us
    unnamed x18, local copies, waits for them, and re-layouts  9.13 us

profile of v2, /device:TPU:3, one launch (start us, length us, event | category | flops | bytes accessed | tf_op | source)
XLA Modules:
  0.0 162.4 jit_solution(15774376652126288733)
XLA Ops:
  0.6 0.0 copy-start.5
  0.7 0.9 convert_reduce_fusion
  1.6 0.7 multiply_add_fusion
  2.3 0.1 fusion
  2.4 0.2 select_reduce_fusion.1
  2.6 0.1 select_n.21
  2.7 0.1 concatenate.6
  2.8 0.0 copy-start.4
  2.9 1.6 copy-done.4
  4.4 31.7 %shard_map.95 = (f32[24,128,128]{2,1,0:T(8,128)S(1)}, f32[2,640,640]{2,1,0:T(8,128)}, s32[8,8,128]{2,1,0:T(8,128)S(1)}) custom-call(s32[2,24]{1,0:T(2,128)S(1)} %get-tuple-element.24.holder, f32[2,24,128,128]{3,2,1,0:T(8,128)} %intensities.3, f32[2,512,512]{2,1,0:T(8,128)S(1)} %copy-done.4, s32[8,8,128]{2,1,0:T(8,128)S(1)} %pad.4.wants), custom_call_target="tpu_custom_call" | custom-call | tf_op jit(solution)/shard_map/pallas_call | solution.py:553
  36.2 0.1 reshape.42
  36.3 0.0 copy-done.5
  36.3 0.0 copy-done.6
  36.3 0.0 copy-done.7
  36.3 1.9 %copy-done.1 = f32[2,640,640]{2,1,0:T(8,128)S(1)} copy-done((f32[2,640,640]{2,1,0:T(8,128)S(1)}, f32[2,640,640]{2,1,0:T(8,128)}, u32[]{:S(2)}) %copy-start.1) | copy-done | bytes 3276824
  38.2 15.3 %shard_map.96 = (f32[2,640,640]{2,1,0:T(8,128)S(1)}, f32[2,128,128]{2,1,0:T(8,128)S(1)}) custom-call(s32[24]{0:T(128)S(1)} %get-tuple-element.26.tops, s32[24]{0:T(128)S(1)} %get-tuple-element.25.lefts, f32[2,640,640]{2,1,0:T(8,128)S(1)} %copy-done.1, f32[2,128,128]{2,1,0:T(8,128)S(1)} %copy-done.5, f32[24,128,128]{2,1,0:T(8,128)S(1)} %get-tuple-element.14.measured, ...), custom_call_target="tpu_custom_call" | custom-call | flops 9663676416 | bytes 8388608 | tf_op jit(solution)/shard_map/pallas_call | solution.py:158
  53.5 0.0 copy-start.2
  53.5 1.7 %copy-done.2 = f32[2,640,640]{2,1,0:T(8,128)} copy-done((f32[2,640,640]{2,1,0:T(8,128)}, f32[2,640,640]{2,1,0:T(8,128)S(1)}, u32[]{:S(2)}) %copy-start.2) | copy-done | bytes 3276824
  55.2 55.5 %shard_map.97 = (f32[24,128,128]{2,1,0:T(8,128)S(1)}, f32[2,640,640]{2,1,0:T(8,128)}, f32[2,128,128]{2,1,0:T(8,128)S(1)}) custom-call(s32[2,24]{1,0:T(2,128)S(1)} %get-tuple-element.24.holder, f32[2,24,128,128]{3,2,1,0:T(8,128)S(1)} %copy-done, f32[2,640,640]{2,1,0:T(8,128)} %copy-done.2, f32[2,128,128]{2,1,0:T(8,128)S(1)} %get-tuple-element.16.probe_term, ...), custom_call_target="tpu_custom_call" | custom-call | tf_op jit(solution)/shard_map/pallas_call | solution.py:573
  110.8 1.9 %copy-done.3 = f32[2,640,640]{2,1,0:T(8,128)S(1)} copy-done((f32[2,640,640]{2,1,0:T(8,128)S(1)}, f32[2,640,640]{2,1,0:T(8,128)}, u32[]{:S(2)}) %copy-start.3) | copy-done | bytes 3276824
  112.7 15.2 %shard_map.98 = (f32[2,640,640]{2,1,0:T(8,128)S(1)}, f32[2,128,128]{2,1,0:T(8,128)S(1)}) custom-call(s32[24]{0:T(128)S(1)} %get-tuple-element.28.tops, s32[24]{0:T(128)S(1)} %get-tuple-element.27.lefts, f32[2,640,640]{2,1,0:T(8,128)S(1)} %copy-done.3, f32[2,128,128]{2,1,0:T(8,128)S(1)} %get-tuple-element.18.probe, ...), custom_call_target="tpu_custom_call" | custom-call | flops 9663676416 | bytes 8388608 | tf_op jit(solution)/shard_map/pallas_call | solution.py:158
  127.9 32.5 %shard_map.99 = (f32[2,512,512]{2,1,0:T(8,128)S(1)}, f32[2,128,128]{2,1,0:T(8,128)S(1)}) custom-call(f32[2,640,640]{2,1,0:T(8,128)S(1)} %get-tuple-element.20.gradient, f32[2,128,128]{2,1,0:T(8,128)S(1)} %get-tuple-element.21.probe_term, f32[2,640,640]{2,1,0:T(8,128)} %get-tuple-element.17.extended, f32[2,128,128]{2,1,0:T(8,128)S(1)} %get-tuple-element.18.probe), custom_call_target="tpu_custom_call" | custom-call | tf_op jit(solution)/shard_map/pallas_call | solution.py:589
  160.4 1.3 copy.25
  161.7 0.7 copy.26
  (15 shorter events, 0.1 us)
Async XLA Ops:
  0.6 35.7 %copy-start.5 = (f32[2,128,128]{2,1,0:T(8,128)S(1)}, f32[2,128,128]{2,1,0:T(8,128)}, u32[]{:S(2)}) copy-start(f32[2,128,128]{2,1,0:T(8,128)} %probe.3) | copy-start | bytes 393220
  2.8 1.6 copy-start.4
  4.4 31.9 %copy-start.6 = (bf16[2,768,256]{2,1,0:T(8,128)(2,1)S(1)}, bf16[2,768,256]{2,1,0:T(8,128)(2,1)}, u32[]{:S(2)}) copy-start(bf16[2,768,256]{2,1,0:T(8,128)(2,1)} %constant.24.clone.right_tables) | copy-start | bytes 2359300
  4.4 31.9 %copy-start.7 = (bf16[2,256,768]{2,1,0:T(8,128)(2,1)S(1)}, bf16[2,256,768]{2,1,0:T(8,128)(2,1)}, u32[]{:S(2)}) copy-start(bf16[2,256,768]{2,1,0:T(8,128)(2,1)} %constant.9.clone.left_tables) | copy-start | bytes 2359300
  36.3 1.9 %copy-start.1 = (f32[2,640,640]{2,1,0:T(8,128)S(1)}, f32[2,640,640]{2,1,0:T(8,128)}, u32[]{:S(2)}) copy-start(f32[2,640,640]{2,1,0:T(8,128)} %get-tuple-element.13.extended) | copy-start | bytes 9830404
  38.2 17.0 %copy-start = (f32[2,24,128,128]{3,2,1,0:T(8,128)S(1)}, f32[2,24,128,128]{3,2,1,0:T(8,128)}, u32[]{:S(2)}) copy-start(f32[2,24,128,128]{3,2,1,0:T(8,128)} %intensities.3) | copy-start | bytes 9437188
  53.5 1.7 %copy-start.2 = (f32[2,640,640]{2,1,0:T(8,128)}, f32[2,640,640]{2,1,0:T(8,128)S(1)}, u32[]{:S(2)}) copy-start(f32[2,640,640]{2,1,0:T(8,128)S(1)} %get-tuple-element.15.gradient) | copy-start | bytes 9830404
  110.7 1.9 %copy-start.3 = (f32[2,640,640]{2,1,0:T(8,128)S(1)}, f32[2,640,640]{2,1,0:T(8,128)}, u32[]{:S(2)}) copy-start(f32[2,640,640]{2,1,0:T(8,128)} %get-tuple-element.17.extended) | copy-start | bytes 9830404

commit v3 on v2

--- a/solution.py
+++ b/solution.py
@@ -141,8 +141,8 @@
             probe_terms = [
                 (qr * br + qi * bi, qr * bi - qi * br) for (qr, qi), (br, bi) in zip(patches, back)
             ]
-            probe_gradient[0] += probe_terms[0][0] + probe_terms[1][0]
-            probe_gradient[1] += probe_terms[0][1] + probe_terms[1][1]
+            probe_gradient[:width] += probe_terms[0][0] + probe_terms[1][0]
+            probe_gradient[width:] += probe_terms[0][1] + probe_terms[1][1]
             for slot, (br, bi) in zip(pair, back):
                 add(slot, (probe_re * br + probe_im * bi, probe_re * bi - probe_im * br))
         return carry
@@ -159,7 +159,7 @@
         step_kernel,
         out_shape=(
             jax.ShapeDtypeStruct(extended.shape, jnp.float32),
-            jax.ShapeDtypeStruct(probe.shape, jnp.float32),
+            jax.ShapeDtypeStruct((2 * width, width), jnp.float32),
         ),
         in_specs=[smem, smem] + [vmem] * 5,
         out_specs=(vmem, vmem),
@@ -314,60 +314,95 @@
         copy.wait()
 
 
-def butterfly(band_count, strip_count, ty, tx):
-    partners = []
-    step = 1
-    while step < strip_count:
-        partners.append(("tx", step, (ty, tx + step * (1 - 2 * (tx // step % 2)))))
-        step *= 2
-    step = 1
-    while step < band_count:
-        partners.append(("ty", step, (ty + step * (1 - 2 * (ty // step % 2)), tx)))
-        step *= 2
-    return partners
-
-
-def probe_rounds(partners, probe_term, sums, arrived, send_sems, recv_sems):
-    def source(k):
-        return probe_term if k == 0 else sums.at[k - 1]
-
-    copies = [
-        remote(source(k), arrived.at[k], send_sems.at[k], recv_sems.at[k], *partner)
-        for k, (_, _, partner) in enumerate(partners)
-    ]
-
-    def finish(k):
-        copies[k].wait()
-        sums[k] = source(k)[...] + arrived[k]
-
-    return copies, finish
+def strip_peers(strip_count, ty, tx):
+    return [(True, ty, lax.rem(tx + k, strip_count)) for k in range(1, strip_count)]
+
+
+class ProbeSum:
+    def __init__(self, sizes, probe_term, total, band_parts, strip_parts, band_sems, strip_sems, share_sems, ty, tx):
+        band_count, strip_count, _ = sizes
+        self.ty, self.tx = ty, tx
+        self.probe_term, self.total = probe_term, total
+        self.band_parts, self.strip_parts = band_parts, strip_parts
+        rows = total.shape[0] // band_count
+        self.mine = pl.ds(ty * rows, rows)
+        self.to_bands, self.to_strips, self.shares = [], [], []
+        for k in range(1, band_count):
+            peer = lax.rem(ty + k, band_count)
+            self.to_bands.append(
+                remote(probe_term.at[pl.ds(peer * rows, rows)], band_parts.at[k - 1],
+                       band_sems.at[0, k - 1], band_sems.at[1, k - 1], peer, tx)
+            )
+            self.shares.append(
+                remote(total.at[self.mine], total.at[self.mine],
+                       share_sems.at[0, k - 1], share_sems.at[1, k - 1], peer, tx)
+            )
+        for k in range(1, strip_count):
+            peer = lax.rem(tx + k, strip_count)
+            self.to_strips.append(
+                remote(strip_parts.at[tx], strip_parts.at[tx],
+                       strip_sems.at[0, k - 1], strip_sems.at[1, k - 1], ty, peer)
+            )
+
+    def start(self):
+        for copy in self.to_bands:
+            copy.start()
+
+    def over_strips(self):
+        for copy in self.to_bands:
+            copy.wait()
+        value = self.probe_term[self.mine, :]
+        for k in range(self.band_parts.shape[0]):
+            value = value + self.band_parts[k]
+        self.strip_parts[self.tx] = value
+        for copy in self.to_strips:
+            copy.start()
+
+    def share(self):
+        for copy in self.to_strips:
+            copy.wait()
+        value = self.strip_parts[0]
+        for k in range(1, self.strip_parts.shape[0]):
+            value = value + self.strip_parts[k]
+        self.total[self.mine, :] = value
+        for copy in self.shares:
+            copy.start()
+
+    def finish(self, scale, probe, new_probe):
+        for copy in self.shares:
+            copy.wait()
+        width = probe.shape[1]
+        for part in range(2):
+            new_probe[part] = probe[part] - scale * self.total[part * width : (part + 1) * width]
 
 
 def middle_kernel(
     sizes, scale, holder, intensities, gradient, probe_term, extended, probe, measured, new_extended, new_probe,
     staged, outgoing, load_sem, send_sems, recv_sems, side, ends, ends_out, side_send, side_recv, end_send, end_recv,
-    sums, arrived, sum_send, sum_recv,
+    total, band_parts, strip_parts, band_sems, strip_sems, share_sems,
 ):
     band_count, strip_count, width = sizes
     ty, tx = lax.axis_index("ty"), lax.axis_index("tx")
     rows, cols = (size - width for size in extended.shape[1:])
     above, left = ty > 0, tx > 0
     below, right = ty < band_count - 1, tx < strip_count - 1
-    partners = butterfly(band_count, strip_count, ty, tx)
     greet(
         peers(band_count, ty, tx)
-        + [(left, ty, tx - 1), (right, ty, tx + 1)]
-        + [(True, *partner) for axis, step, partner in partners if axis == "tx" and step > 1]
-    )
-    copies, finish = probe_rounds(partners, probe_term, sums, arrived, sum_send, sum_recv)
-    copies[0].start()
+        + strip_peers(strip_count, ty, tx)
+    )
+    probe_sum = ProbeSum(
+        sizes, probe_term, total, band_parts, strip_parts, band_sems, strip_sems, share_sems, ty, tx
+    )
+    probe_sum.start()
     sides = [
         (right, left, remote(gradient.at[:, :, cols:], side.at[0], side_send.at[0], side_recv.at[0], ty, tx + 1)),
         (left, right, remote(gradient.at[:, :, :width], side.at[1], side_send.at[1], side_recv.at[1], ty, tx - 1)),
     ]
+    stage_measured(1, intensities, holder, staged, outgoing, measured, load_sem, ty)
+    probe_sum.over_strips()
     for sends, _, copy in sides:
         only(sends)(copy.start)
-    stage_measured(1, intensities, holder, staged, outgoing, measured, load_sem, ty)
+    probe_sum.share()
     measured_sends = measured_copies(band_count, outgoing, measured, send_sems, recv_sems, ty, tx)
     for copy in measured_sends:
         copy.start()
@@ -377,11 +412,6 @@
         def _(number=number):
             side[number] = jnp.zeros(side.shape[1:], jnp.float32)
 
-    for k in range(len(copies)):
-        finish(k)
-        if k + 1 < len(copies):
-            copies[k + 1].start()
-    new_probe[...] = probe[...] - scale * sums[len(copies) - 1]
     for sends, receives, copy in sides:
         only(sends)(copy.wait_send)
         only(receives)(copy.wait_recv)
@@ -417,33 +447,30 @@
         only(receives)(copy.wait_recv)
     new_extended[:, :width, :] = extended[:, :width, :] - OBJECT_RATE * (ends_out[1] + ends[0])
     new_extended[:, rows:, :] = extended[:, rows:, :] - OBJECT_RATE * (ends_out[0] + ends[1])
+    probe_sum.finish(scale, probe, new_probe)
     for copy in measured_sends:
         copy.wait()
 
 
 def end_kernel(
     sizes, scale, gradient, probe_term, extended, probe, new_object, new_probe,
-    side, end, corner, halo_send, halo_recv, sums, arrived, sum_send, sum_recv,
+    side, end, corner, halo_send, halo_recv,
+    total, band_parts, strip_parts, band_sems, strip_sems, share_sems,
 ):
     band_count, strip_count, width = sizes
     ty, tx = lax.axis_index("ty"), lax.axis_index("tx")
     rows, cols = new_object.shape[1:]
     above, left = ty > 0, tx > 0
     below, right = ty < band_count - 1, tx < strip_count - 1
-    partners = butterfly(band_count, strip_count, ty, tx)
     greet(
-        [
-            (left, ty, tx - 1),
-            (right, ty, tx + 1),
-            (above, ty - 1, tx),
-            (below, ty + 1, tx),
-            (above & left, ty - 1, tx - 1),
-            (below & right, ty + 1, tx + 1),
-        ]
-        + [(True, *partner) for _, step, partner in partners if step > 1]
-    )
-    copies, finish = probe_rounds(partners, probe_term, sums, arrived, sum_send, sum_recv)
-    copies[0].start()
+        peers(band_count, ty, tx)
+        + strip_peers(strip_count, ty, tx)
+        + [(above & left, ty - 1, tx - 1), (below & right, ty + 1, tx + 1)]
+    )
+    probe_sum = ProbeSum(
+        sizes, probe_term, total, band_parts, strip_parts, band_sems, strip_sems, share_sems, ty, tx
+    )
+    probe_sum.start()
     halos = [
         (right, left, side, remote(gradient.at[:, :rows, cols:], side, halo_send.at[0], halo_recv.at[0], ty, tx + 1)),
         (below, above, end, remote(gradient.at[:, rows:, :cols], end, halo_send.at[1], halo_recv.at[1], ty + 1, tx)),
@@ -452,8 +479,11 @@
             remote(gradient.at[:, rows:, cols:], corner, halo_send.at[2], halo_recv.at[2], ty + 1, tx + 1),
         ),
     ]
-    for sends, _, _, copy in halos:
-        only(sends)(copy.start)
+    only(halos[1][0])(halos[1][3].start)
+    probe_sum.over_strips()
+    only(halos[0][0])(halos[0][3].start)
+    only(halos[2][0])(halos[2][3].start)
+    probe_sum.share()
     for _, receives, target, _ in halos:
 
         @only(jnp.logical_not(receives))
@@ -463,11 +493,7 @@
     new_object[:, width:, width:] = (
         extended[:, width:rows, width:cols] - OBJECT_RATE * gradient[:, width:rows, width:cols]
     )
-    for k in range(len(copies)):
-        finish(k)
-        if k + 1 < len(copies):
-            copies[k + 1].start()
-    new_probe[...] = probe[...] - scale * sums[len(copies) - 1]
+    probe_sum.finish(scale, probe, new_probe)
     for sends, receives, _, copy in halos:
         only(sends)(copy.wait_send)
         only(receives)(copy.wait_recv)
@@ -562,12 +588,14 @@
         staging + [DMA] + pair_sems + pair_sems + [DMA((3,)), DMA((3,))],
     )(holder, intensities, object_field, wants)
     received = received[:, : 2 * STEPS, :CAP].transpose(1, 0, 2).reshape(2, STEPS, slot_count)
-    rounds = (band_count * strip_count).bit_length() - 1
+    share_rows = 2 * width // band_count
     summing = [
-        pltpu.VMEM((rounds, 2, width, width), jnp.float32),
-        pltpu.VMEM((rounds, 2, width, width), jnp.float32),
-        DMA((rounds,)),
-        DMA((rounds,)),
+        pltpu.VMEM((2 * width, width), jnp.float32),
+        pltpu.VMEM((band_count - 1, share_rows, width), jnp.float32),
+        pltpu.VMEM((strip_count, share_rows, width), jnp.float32),
+        DMA((2, band_count - 1)),
+        DMA((2, strip_count - 1)),
+        DMA((2, band_count - 1)),
     ]
     gradient, probe_term = run_step(received[0, 0], received[1, 0], extended, probe_field, measured, tables)
     measured, extended, probe_field = communicate(

time: 164 us -> 148 us (0.902)
  Pallas kernels: 150 us -> 133 us
    pallas_call x1, Pallas kernels: 32.5 us -> 22.9 us  [on_device(): communicate(functools.partial(end_kernel, sizes, probe_scale), 2, [VMEM]...]
    pallas_call x1, Pallas kernels: 55.5 us -> 48 us  [on_device(): communicate(functools.partial(middle_kernel, sizes, probe_scale), 1, [SME...]
where the time goes in v3:
time: 148 us; the launch traced here: 145 us
  Pallas kernels  133 us (90%)
  local copies, waits for them, and re-layouts  9.4 us (6%)
  other arithmetic  1.99 us (1%)
    pallas_call x1, Pallas kernels, on_device(): communicate(functools.partial(middle_kernel, sizes, probe_scale), 1, [SME...  48 us
    pallas_call x1, Pallas kernels, on_device(): communicate(functools.partial(begin_kernel, sizes), 0, [SMEM, HBM, HBM, V...  31.7 us
    pallas_call x2, Pallas kernels, run_step(): pl.pallas_call(step_kernel, out_shape=(jax.ShapeDtypeStruct(extended.shap...  30.5 us
    pallas_call x1, Pallas kernels, on_device(): communicate(functools.partial(end_kernel, sizes, probe_scale), 2, [VMEM]...  22.9 us
    unnamed x18, local copies, waits for them, and re-layouts  9.13 us

profile of v3, /device:TPU:3, one launch (start us, length us, event | category | flops | bytes accessed | tf_op | source)
XLA Modules:
  0.0 145.3 jit_solution(1417370170363681239)
XLA Ops:
  0.6 0.0 copy-start.5
  0.7 0.9 convert_reduce_fusion
  1.6 0.7 multiply_add_fusion
  2.3 0.1 fusion
  2.4 0.2 select_reduce_fusion.1
  2.6 0.1 select_n.21
  2.7 0.1 concatenate.6
  2.8 0.0 copy-start.4
  2.9 1.6 %copy-done.4 = f32[2,512,512]{2,1,0:T(8,128)S(1)} copy-done((f32[2,512,512]{2,1,0:T(8,128)S(1)}, f32[2,512,512]{2,1,0:T(8,128)}, u32[]{:S(2)}) %copy-start.4) | copy-done | bytes 2097176
  4.4 31.7 %shard_map.95 = (f32[24,128,128]{2,1,0:T(8,128)S(1)}, f32[2,640,640]{2,1,0:T(8,128)}, s32[8,8,128]{2,1,0:T(8,128)S(1)}) custom-call(s32[2,24]{1,0:T(2,128)S(1)} %get-tuple-element.24.holder, f32[2,24,128,128]{3,2,1,0:T(8,128)} %intensities.3, f32[2,512,512]{2,1,0:T(8,128)S(1)} %copy-done.4, s32[8,8,128]{2,1,0:T(8,128)S(1)} %pad.4.wants), custom_call_target="tpu_custom_call" | custom-call | tf_op jit(solution)/shard_map/pallas_call | solution.py:579
  36.2 0.1 reshape.42
  36.3 0.0 copy-done.5
  36.3 0.0 copy-done.6
  36.3 1.9 %copy-done.1 = f32[2,640,640]{2,1,0:T(8,128)S(1)} copy-done((f32[2,640,640]{2,1,0:T(8,128)S(1)}, f32[2,640,640]{2,1,0:T(8,128)}, u32[]{:S(2)}) %copy-start.1) | copy-done | bytes 3276824
  38.2 15.3 %shard_map.96 = (f32[2,640,640]{2,1,0:T(8,128)S(1)}, f32[256,128]{1,0:T(8,128)S(1)}) custom-call(s32[24]{0:T(128)S(1)} %get-tuple-element.26.tops, s32[24]{0:T(128)S(1)} %get-tuple-element.25.lefts, f32[2,640,640]{2,1,0:T(8,128)S(1)} %copy-done.1, f32[2,128,128]{2,1,0:T(8,128)S(1)} %copy-done.5, f32[24,128,128]{2,1,0:T(8,128)S(1)} %get-tuple-element.14.measured, ...), custom_call_target="tpu_custom_call" | custom-call | flops 9663676416 | bytes 8388608 | tf_op jit(solution)/shard_map/pallas_call | solution.py:158
  53.5 0.0 copy-start.2
  53.5 1.7 %copy-done.2 = f32[2,640,640]{2,1,0:T(8,128)} copy-done((f32[2,640,640]{2,1,0:T(8,128)}, f32[2,640,640]{2,1,0:T(8,128)S(1)}, u32[]{:S(2)}) %copy-start.2) | copy-done | bytes 3276824
  55.2 48.0 %shard_map.97 = (f32[24,128,128]{2,1,0:T(8,128)S(1)}, f32[2,640,640]{2,1,0:T(8,128)}, f32[2,128,128]{2,1,0:T(8,128)S(1)}) custom-call(s32[2,24]{1,0:T(2,128)S(1)} %get-tuple-element.24.holder, f32[2,24,128,128]{3,2,1,0:T(8,128)S(1)} %copy-done, f32[2,640,640]{2,1,0:T(8,128)} %copy-done.2, f32[256,128]{1,0:T(8,128)S(1)} %get-tuple-element.16.probe_term, ...), custom_call_target="tpu_custom_call" | custom-call | tf_op jit(solution)/shard_map/pallas_call | solution.py:601
  103.3 0.0 copy-start.3
  103.3 1.9 %copy-done.3 = f32[2,640,640]{2,1,0:T(8,128)S(1)} copy-done((f32[2,640,640]{2,1,0:T(8,128)S(1)}, f32[2,640,640]{2,1,0:T(8,128)}, u32[]{:S(2)}) %copy-start.3) | copy-done | bytes 3276824
  105.2 15.2 %shard_map.98 = (f32[2,640,640]{2,1,0:T(8,128)S(1)}, f32[256,128]{1,0:T(8,128)S(1)}) custom-call(s32[24]{0:T(128)S(1)} %get-tuple-element.28.tops, s32[24]{0:T(128)S(1)} %get-tuple-element.27.lefts, f32[2,640,640]{2,1,0:T(8,128)S(1)} %copy-done.3, f32[2,128,128]{2,1,0:T(8,128)S(1)} %get-tuple-element.18.probe, ...), custom_call_target="tpu_custom_call" | custom-call | flops 9663676416 | bytes 8388608 | tf_op jit(solution)/shard_map/pallas_call | solution.py:158
  120.4 22.9 %shard_map.99 = (f32[2,512,512]{2,1,0:T(8,128)S(1)}, f32[2,128,128]{2,1,0:T(8,128)S(1)}) custom-call(f32[2,640,640]{2,1,0:T(8,128)S(1)} %get-tuple-element.20.gradient, f32[256,128]{1,0:T(8,128)S(1)} %get-tuple-element.21.probe_term, f32[2,640,640]{2,1,0:T(8,128)} %get-tuple-element.17.extended, f32[2,128,128]{2,1,0:T(8,128)S(1)} %get-tuple-element.18.probe), custom_call_target="tpu_custom_call" | custom-call | tf_op jit(solution)/shard_map/pallas_call | solution.py:617
  143.3 1.3 copy.25
  144.6 0.7 copy.26
  (15 shorter events, 0.1 us)
Async XLA Ops:
  0.6 35.7 %copy-start.5 = (f32[2,128,128]{2,1,0:T(8,128)S(1)}, f32[2,128,128]{2,1,0:T(8,128)}, u32[]{:S(2)}) copy-start(f32[2,128,128]{2,1,0:T(8,128)} %probe.3) | copy-start | bytes 393220
  2.8 1.6 %copy-start.4 = (f32[2,512,512]{2,1,0:T(8,128)S(1)}, f32[2,512,512]{2,1,0:T(8,128)}, u32[]{:S(2)}) copy-start(f32[2,512,512]{2,1,0:T(8,128)} %object_field.1) | copy-start | bytes 6291460
  4.4 31.9 %copy-start.6 = (bf16[2,768,256]{2,1,0:T(8,128)(2,1)S(1)}, bf16[2,768,256]{2,1,0:T(8,128)(2,1)}, u32[]{:S(2)}) copy-start(bf16[2,768,256]{2,1,0:T(8,128)(2,1)} %constant.24.clone.right_tables) | copy-start | bytes 2359300
  4.4 31.9 %copy-start.7 = (bf16[2,256,768]{2,1,0:T(8,128)(2,1)S(1)}, bf16[2,256,768]{2,1,0:T(8,128)(2,1)}, u32[]{:S(2)}) copy-start(bf16[2,256,768]{2,1,0:T(8,128)(2,1)} %constant.9.clone.left_tables) | copy-start | bytes 2359300
  36.3 1.9 %copy-start.1 = (f32[2,640,640]{2,1,0:T(8,128)S(1)}, f32[2,640,640]{2,1,0:T(8,128)}, u32[]{:S(2)}) copy-start(f32[2,640,640]{2,1,0:T(8,128)} %get-tuple-element.13.extended) | copy-start | bytes 9830404
  38.2 17.0 %copy-start = (f32[2,24,128,128]{3,2,1,0:T(8,128)S(1)}, f32[2,24,128,128]{3,2,1,0:T(8,128)}, u32[]{:S(2)}) copy-start(f32[2,24,128,128]{3,2,1,0:T(8,128)} %intensities.3) | copy-start | bytes 9437188
  53.5 1.7 %copy-start.2 = (f32[2,640,640]{2,1,0:T(8,128)}, f32[2,640,640]{2,1,0:T(8,128)S(1)}, u32[]{:S(2)}) copy-start(f32[2,640,640]{2,1,0:T(8,128)S(1)} %get-tuple-element.15.gradient) | copy-start | bytes 9830404
  103.3 1.9 %copy-start.3 = (f32[2,640,640]{2,1,0:T(8,128)S(1)}, f32[2,640,640]{2,1,0:T(8,128)}, u32[]{:S(2)}) copy-start(f32[2,640,640]{2,1,0:T(8,128)} %get-tuple-element.17.extended) | copy-start | bytes 9830404

commit v4 on v3

--- a/solution.py
+++ b/solution.py
@@ -12,7 +12,8 @@
 
 CAP = 3
 STEPS = 2
-GROUP = 4
+GROUP = 8
+JOINT = 8
 ROWS = 8
 
 OBJECT_RATE = 0.25
@@ -123,7 +124,7 @@
 
     def body(group, carry):
         pairs = [
-            [group * GROUP + 2 * pair, group * GROUP + 2 * pair + 1] for pair in range(GROUP // 2)
+            [group * GROUP + JOINT * pair + i for i in range(JOINT)] for pair in range(GROUP // JOINT)
         ]
         for pair in pairs:
             patches = [cut(slot) for slot in pair]
@@ -141,8 +142,8 @@
             probe_terms = [
                 (qr * br + qi * bi, qr * bi - qi * br) for (qr, qi), (br, bi) in zip(patches, back)
             ]
-            probe_gradient[:width] += probe_terms[0][0] + probe_terms[1][0]
-            probe_gradient[width:] += probe_terms[0][1] + probe_terms[1][1]
+            probe_gradient[:width] += sum(re for re, _ in probe_terms)
+            probe_gradient[width:] += sum(im for _, im in probe_terms)
             for slot, (br, bi) in zip(pair, back):
                 add(slot, (probe_re * br + probe_im * bi, probe_re * bi - probe_im * br))
         return carry

time: 148 us -> 138 us (0.932)
  Pallas kernels: 133 us -> 124 us
    pallas_call x2, Pallas kernels: 30.5 us -> 20.8 us  [run_step(): pl.pallas_call(step_kernel, out_shape=(jax.ShapeDtypeStruct(extended.shap...]
where the time goes in v4:
time: 138 us; the launch traced here: 136 us
  Pallas kernels  124 us (90%)
  local copies, waits for them, and re-layouts  9.4 us (7%)
  other arithmetic  1.99 us (1%)
    pallas_call x1, Pallas kernels, on_device(): communicate(functools.partial(middle_kernel, sizes, probe_scale), 1, [SME...  48.2 us
    pallas_call x1, Pallas kernels, on_device(): communicate(functools.partial(begin_kernel, sizes), 0, [SMEM, HBM, HBM, V...  31.7 us
    pallas_call x1, Pallas kernels, on_device(): communicate(functools.partial(end_kernel, sizes, probe_scale), 2, [VMEM]...  22.9 us
    pallas_call x2, Pallas kernels, run_step(): pl.pallas_call(step_kernel, out_shape=(jax.ShapeDtypeStruct(extended.shap...  20.8 us
    unnamed x18, local copies, waits for them, and re-layouts  9.13 us

profile of v4, /device:TPU:3, one launch (start us, length us, event | category | flops | bytes accessed | tf_op | source)
XLA Modules:
  0.0 135.7 jit_solution(14837292359573980666)
XLA Ops:
  0.6 0.0 copy-start.5
  0.7 0.9 convert_reduce_fusion
  1.6 0.7 multiply_add_fusion
  2.3 0.1 fusion
  2.4 0.2 select_reduce_fusion.1
  2.6 0.1 select_n.21
  2.7 0.1 concatenate.6
  2.8 0.0 copy-start.4
  2.9 1.6 %copy-done.4 = f32[2,512,512]{2,1,0:T(8,128)S(1)} copy-done((f32[2,512,512]{2,1,0:T(8,128)S(1)}, f32[2,512,512]{2,1,0:T(8,128)}, u32[]{:S(2)}) %copy-start.4) | copy-done | bytes 2097176
  4.4 31.7 %shard_map.95 = (f32[24,128,128]{2,1,0:T(8,128)S(1)}, f32[2,640,640]{2,1,0:T(8,128)}, s32[8,8,128]{2,1,0:T(8,128)S(1)}) custom-call(s32[2,24]{1,0:T(2,128)S(1)} %get-tuple-element.24.holder, f32[2,24,128,128]{3,2,1,0:T(8,128)} %intensities.3, f32[2,512,512]{2,1,0:T(8,128)S(1)} %copy-done.4, s32[8,8,128]{2,1,0:T(8,128)S(1)} %pad.4.wants), custom_call_target="tpu_custom_call" | custom-call | tf_op jit(solution)/shard_map/pallas_call | solution.py:580
  36.2 0.1 reshape.42
  36.3 0.0 copy-done.6
  36.3 0.0 copy-done.7
  36.3 0.0 copy-start.1
  36.3 1.9 %copy-done.1 = f32[2,640,640]{2,1,0:T(8,128)S(1)} copy-done((f32[2,640,640]{2,1,0:T(8,128)S(1)}, f32[2,640,640]{2,1,0:T(8,128)}, u32[]{:S(2)}) %copy-start.1) | copy-done | bytes 3276824
  38.2 10.4 %shard_map.96 = (f32[2,640,640]{2,1,0:T(8,128)S(1)}, f32[256,128]{1,0:T(8,128)S(1)}) custom-call(s32[24]{0:T(128)S(1)} %get-tuple-element.26.tops, s32[24]{0:T(128)S(1)} %get-tuple-element.25.lefts, f32[2,640,640]{2,1,0:T(8,128)S(1)} %copy-done.1, f32[2,128,128]{2,1,0:T(8,128)S(1)} %copy-done.5, f32[24,128,128]{2,1,0:T(8,128)S(1)} %get-tuple-element.14.measured, ...), custom_call_target="tpu_custom_call" | custom-call | flops 9663676416 | bytes 8388608 | tf_op jit(solution)/shard_map/pallas_call | solution.py:159
  48.7 1.7 %copy-done.2 = f32[2,640,640]{2,1,0:T(8,128)} copy-done((f32[2,640,640]{2,1,0:T(8,128)}, f32[2,640,640]{2,1,0:T(8,128)S(1)}, u32[]{:S(2)}) %copy-start.2) | copy-done | bytes 3276824
  50.4 48.2 %shard_map.97 = (f32[24,128,128]{2,1,0:T(8,128)S(1)}, f32[2,640,640]{2,1,0:T(8,128)}, f32[2,128,128]{2,1,0:T(8,128)S(1)}) custom-call(s32[2,24]{1,0:T(2,128)S(1)} %get-tuple-element.24.holder, f32[2,24,128,128]{3,2,1,0:T(8,128)S(1)} %copy-done, f32[2,640,640]{2,1,0:T(8,128)} %copy-done.2, f32[256,128]{1,0:T(8,128)S(1)} %get-tuple-element.16.probe_term, ...), custom_call_target="tpu_custom_call" | custom-call | tf_op jit(solution)/shard_map/pallas_call | solution.py:602
  98.6 0.0 copy-start.3
  98.6 1.9 %copy-done.3 = f32[2,640,640]{2,1,0:T(8,128)S(1)} copy-done((f32[2,640,640]{2,1,0:T(8,128)S(1)}, f32[2,640,640]{2,1,0:T(8,128)}, u32[]{:S(2)}) %copy-start.3) | copy-done | bytes 3276824
  100.5 10.4 %shard_map.98 = (f32[2,640,640]{2,1,0:T(8,128)S(1)}, f32[256,128]{1,0:T(8,128)S(1)}) custom-call(s32[24]{0:T(128)S(1)} %get-tuple-element.28.tops, s32[24]{0:T(128)S(1)} %get-tuple-element.27.lefts, f32[2,640,640]{2,1,0:T(8,128)S(1)} %copy-done.3, f32[2,128,128]{2,1,0:T(8,128)S(1)} %get-tuple-element.18.probe, ...), custom_call_target="tpu_custom_call" | custom-call | flops 9663676416 | bytes 8388608 | tf_op jit(solution)/shard_map/pallas_call | solution.py:159
  110.9 22.9 %shard_map.99 = (f32[2,512,512]{2,1,0:T(8,128)S(1)}, f32[2,128,128]{2,1,0:T(8,128)S(1)}) custom-call(f32[2,640,640]{2,1,0:T(8,128)S(1)} %get-tuple-element.20.gradient, f32[256,128]{1,0:T(8,128)S(1)} %get-tuple-element.21.probe_term, f32[2,640,640]{2,1,0:T(8,128)} %get-tuple-element.17.extended, f32[2,128,128]{2,1,0:T(8,128)S(1)} %get-tuple-element.18.probe), custom_call_target="tpu_custom_call" | custom-call | tf_op jit(solution)/shard_map/pallas_call | solution.py:618
  133.7 1.3 copy.25
  135.1 0.7 copy.26
  (15 shorter events, 0.1 us)
Async XLA Ops:
  0.6 35.7 %copy-start.5 = (f32[2,128,128]{2,1,0:T(8,128)S(1)}, f32[2,128,128]{2,1,0:T(8,128)}, u32[]{:S(2)}) copy-start(f32[2,128,128]{2,1,0:T(8,128)} %probe.3) | copy-start | bytes 393220
  2.8 1.6 %copy-start.4 = (f32[2,512,512]{2,1,0:T(8,128)S(1)}, f32[2,512,512]{2,1,0:T(8,128)}, u32[]{:S(2)}) copy-start(f32[2,512,512]{2,1,0:T(8,128)} %object_field.1) | copy-start | bytes 6291460
  4.4 31.9 %copy-start.6 = (bf16[2,768,256]{2,1,0:T(8,128)(2,1)S(1)}, bf16[2,768,256]{2,1,0:T(8,128)(2,1)}, u32[]{:S(2)}) copy-start(bf16[2,768,256]{2,1,0:T(8,128)(2,1)} %constant.24.clone.right_tables) | copy-start | bytes 2359300
  4.4 31.9 %copy-start.7 = (bf16[2,256,768]{2,1,0:T(8,128)(2,1)S(1)}, bf16[2,256,768]{2,1,0:T(8,128)(2,1)}, u32[]{:S(2)}) copy-start(bf16[2,256,768]{2,1,0:T(8,128)(2,1)} %constant.9.clone.left_tables) | copy-start | bytes 2359300
  36.3 1.9 %copy-start.1 = (f32[2,640,640]{2,1,0:T(8,128)S(1)}, f32[2,640,640]{2,1,0:T(8,128)}, u32[]{:S(2)}) copy-start(f32[2,640,640]{2,1,0:T(8,128)} %get-tuple-element.13.extended) | copy-start | bytes 9830404
  38.2 12.1 %copy-start = (f32[2,24,128,128]{3,2,1,0:T(8,128)S(1)}, f32[2,24,128,128]{3,2,1,0:T(8,128)}, u32[]{:S(2)}) copy-start(f32[2,24,128,128]{3,2,1,0:T(8,128)} %intensities.3) | copy-start | bytes 9437188
  48.6 1.7 %copy-start.2 = (f32[2,640,640]{2,1,0:T(8,128)}, f32[2,640,640]{2,1,0:T(8,128)S(1)}, u32[]{:S(2)}) copy-start(f32[2,640,640]{2,1,0:T(8,128)S(1)} %get-tuple-element.15.gradient) | copy-start | bytes 9830404
  98.6 1.9 %copy-start.3 = (f32[2,640,640]{2,1,0:T(8,128)S(1)}, f32[2,640,640]{2,1,0:T(8,128)}, u32[]{:S(2)}) copy-start(f32[2,640,640]{2,1,0:T(8,128)} %get-tuple-element.17.extended) | copy-start | bytes 9830404

commit v5 on v4

--- a/solution.py
+++ b/solution.py
@@ -166,7 +166,7 @@
         out_specs=(vmem, vmem),
         compiler_params=pltpu.CompilerParams(vmem_limit_bytes=40 * 1024 * 1024),
         cost_estimate=pl.CostEstimate(
-            flops=slots * 24 * 8 * width**3, bytes_accessed=8 * 1024 * 1024, transcendentals=0
+            flops=slots * 24 * 32 * width**3, bytes_accessed=8 * 1024 * 1024, transcendentals=0
         ),
     )(tops, lefts, extended, probe, measured, *tables)
 
@@ -378,8 +378,8 @@
 
 
 def middle_kernel(
-    sizes, scale, holder, intensities, gradient, probe_term, extended, probe, measured, new_extended, new_probe,
-    staged, outgoing, load_sem, send_sems, recv_sems, side, ends, ends_out, side_send, side_recv, end_send, end_recv,
+    sizes, scale, gradient, probe_term, extended, probe, new_extended, new_probe,
+    side, ends, corners, side_send, side_recv, end_send, end_recv, corner_send, corner_recv,
     total, band_parts, strip_parts, band_sems, strip_sems, share_sems,
 ):
     band_count, strip_count, width = sizes
@@ -387,9 +387,16 @@
     rows, cols = (size - width for size in extended.shape[1:])
     above, left = ty > 0, tx > 0
     below, right = ty < band_count - 1, tx < strip_count - 1
+    diagonals = [
+        (below & right, above & left, 1, 1),
+        (below & left, above & right, 1, -1),
+        (above & right, below & left, -1, 1),
+        (above & left, below & right, -1, -1),
+    ]
     greet(
         peers(band_count, ty, tx)
         + strip_peers(strip_count, ty, tx)
+        + [(sends, ty + down, tx + across) for sends, _, down, across in diagonals]
     )
     probe_sum = ProbeSum(
         sizes, probe_term, total, band_parts, strip_parts, band_sems, strip_sems, share_sems, ty, tx
@@ -399,58 +406,55 @@
         (right, left, remote(gradient.at[:, :, cols:], side.at[0], side_send.at[0], side_recv.at[0], ty, tx + 1)),
         (left, right, remote(gradient.at[:, :, :width], side.at[1], side_send.at[1], side_recv.at[1], ty, tx - 1)),
     ]
-    stage_measured(1, intensities, holder, staged, outgoing, measured, load_sem, ty)
+    end_copies = [
+        (below, above, remote(gradient.at[:, rows:, :], ends.at[0], end_send.at[0], end_recv.at[0], ty + 1, tx)),
+        (above, below, remote(gradient.at[:, :width, :], ends.at[1], end_send.at[1], end_recv.at[1], ty - 1, tx)),
+    ]
+    corner_copies = []
+    for number, (sends, receives, down, across) in enumerate(diagonals):
+        block = gradient.at[:, pl.ds(rows if down > 0 else 0, width), pl.ds(cols if across > 0 else 0, width)]
+        corner_copies.append(
+            (
+                sends, receives,
+                remote(block, corners.at[number], corner_send.at[number], corner_recv.at[number],
+                       ty + down, tx + across),
+            )
+        )
+    bulk = sides + end_copies + corner_copies
+    targets = [side.at[0], side.at[1], ends.at[0], ends.at[1]] + [corners.at[number] for number in range(4)]
     probe_sum.over_strips()
-    for sends, _, copy in sides:
+    for sends, _, copy in bulk:
         only(sends)(copy.start)
     probe_sum.share()
-    measured_sends = measured_copies(band_count, outgoing, measured, send_sems, recv_sems, ty, tx)
-    for copy in measured_sends:
-        copy.start()
-    for number, (_, receives, _) in enumerate(sides):
+    for (_, receives, _), target in zip(bulk, targets):
 
         @only(jnp.logical_not(receives))
-        def _(number=number):
-            side[number] = jnp.zeros(side.shape[1:], jnp.float32)
-
-    for sends, receives, copy in sides:
+        def _(target=target):
+            target[...] = jnp.zeros(target.shape, jnp.float32)
+
+    inner = slice(width, rows)
+    middle = slice(width, cols)
+    new_extended[:, inner, middle] = extended[:, inner, middle] - OBJECT_RATE * gradient[:, inner, middle]
+    for sends, receives, copy in bulk:
         only(sends)(copy.wait_send)
         only(receives)(copy.wait_recv)
-    for number, first in enumerate((rows, 0)):
-        block = pl.ds(first, width)
-        ends_out[number, :, :, :width] = gradient[:, block, :width] + side[0, :, block, :]
-        ends_out[number, :, :, width:cols] = gradient[:, block, width:cols]
-        ends_out[number, :, :, cols:] = gradient[:, block, cols:] + side[1, :, block, :]
-    end_copies = [
-        (below, above, remote(ends_out.at[0], ends.at[0], end_send.at[0], end_recv.at[0], ty + 1, tx)),
-        (above, below, remote(ends_out.at[1], ends.at[1], end_send.at[1], end_recv.at[1], ty - 1, tx)),
-    ]
-    for sends, _, copy in end_copies:
-        only(sends)(copy.start)
-    for number, (_, receives, _) in enumerate(end_copies):
-
-        @only(jnp.logical_not(receives))
-        def _(number=number):
-            ends[number] = jnp.zeros(ends.shape[1:], jnp.float32)
-
-    inner = pl.ds(width, rows - width)
-    new_extended[:, inner, :width] = extended[:, inner, :width] - OBJECT_RATE * (
-        gradient[:, inner, :width] + side[0, :, inner, :]
-    )
-    new_extended[:, inner, width:cols] = (
-        extended[:, inner, width:cols] - OBJECT_RATE * gradient[:, inner, width:cols]
-    )
-    new_extended[:, inner, cols:] = extended[:, inner, cols:] - OBJECT_RATE * (
-        gradient[:, inner, cols:] + side[1, :, inner, :]
-    )
-    for sends, receives, copy in end_copies:
-        only(sends)(copy.wait_send)
-        only(receives)(copy.wait_recv)
-    new_extended[:, :width, :] = extended[:, :width, :] - OBJECT_RATE * (ends_out[1] + ends[0])
-    new_extended[:, rows:, :] = extended[:, rows:, :] - OBJECT_RATE * (ends_out[0] + ends[1])
+    first, last = slice(0, width), slice(cols, cols + width)
+    for number, lanes in enumerate((first, last)):
+        new_extended[:, inner, lanes] = extended[:, inner, lanes] - OBJECT_RATE * (
+            gradient[:, inner, lanes] + side[number, :, inner, :]
+        )
+    for number, block in enumerate((slice(0, width), slice(rows, rows + width))):
+        new_extended[:, block, middle] = extended[:, block, middle] - OBJECT_RATE * (
+            gradient[:, block, middle] + ends[number, :, :, middle]
+        )
+        for edge, lanes in enumerate((first, last)):
+            new_extended[:, block, lanes] = extended[:, block, lanes] - OBJECT_RATE * (
+                gradient[:, block, lanes]
+                + ends[number, :, :, lanes]
+                + side[edge, :, block, :]
+                + corners[2 * number + edge]
+            )
     probe_sum.finish(scale, probe, new_probe)
-    for copy in measured_sends:
-        copy.wait()
 
 
 def end_kernel(
@@ -598,23 +602,31 @@
         DMA((2, strip_count - 1)),
         DMA((2, band_count - 1)),
     ]
+    later, _ = lax.optimization_barrier(
+        (
+            jnp.take(intensities.reshape(-1, width, width), holder[1] + batch_rows, axis=0, mode="clip"),
+            received,
+        )
+    )
+    later = lax.all_to_all(
+        later.reshape(band_count, CAP, width, width), "ty", split_axis=0, concat_axis=0, tiled=True
+    ).reshape(slot_count, width, width)
     gradient, probe_term = run_step(received[0, 0], received[1, 0], extended, probe_field, measured, tables)
-    measured, extended, probe_field = communicate(
+    extended, probe_field = communicate(
         functools.partial(middle_kernel, sizes, probe_scale),
         1,
-        [SMEM, HBM] + [VMEM] * 4,
-        (floats(*measured.shape), floats(*extended.shape), floats(*probe_field.shape)),
-        staging
-        + pair_sems
-        + [
+        [VMEM] * 4,
+        (floats(*extended.shape), floats(*probe_field.shape)),
+        [
             pltpu.VMEM((2, 2, tile_rows + width, width), jnp.float32),
             pltpu.VMEM((2, 2, width, tile_cols + width), jnp.float32),
-            pltpu.VMEM((2, 2, width, tile_cols + width), jnp.float32),
+            pltpu.VMEM((4, 2, width, width), jnp.float32),
         ]
         + [DMA((2,))] * 4
+        + [DMA((4,))] * 2
         + summing,
-    )(holder, intensities, gradient, probe_term, extended, probe_field)
-    gradient, probe_term = run_step(received[0, 1], received[1, 1], extended, probe_field, measured, tables)
+    )(gradient, probe_term, extended, probe_field)
+    gradient, probe_term = run_step(received[0, 1], received[1, 1], extended, probe_field, later, tables)
     return communicate(
         functools.partial(end_kernel, sizes, probe_scale),
         2,

time: 138 us -> 136 us (0.986)
  Pallas kernels: 124 us -> 109 us
  local copies, waits for them, and re-layouts: 9.4 us -> 17.1 us
  starting transfers between devices: 0 us -> 4.38 us
    pallas_call x1, Pallas kernels: 48.2 us -> 32.3 us  [on_device(): communicate(functools.partial(middle_kernel, sizes, probe_scale), 1, [VME...]
    all_to_all x0 -> x1, starting transfers between devices: none -> 4.38 us  [on_device(): lax.all_to_all(later.reshape(band_count, CAP, width, width), 'ty', split_...]
    gather x0 -> x1, local copies, waits for them, and re-layouts: none -> 3.93 us  [on_device(): jnp.take(intensities.reshape(-1, width, width), holder[1] + batch_rows, a...]
    unnamed x18 -> x24, local copies, waits for them, and re-layouts: 9.13 us -> 12.9 us
  transfers between devices with their start and end apart: 0 -> 1, of which waited for: 0 -> 0; matrix products, arithmetic and copies ran while one was open for 0% -> 0% of each run, Pallas kernels for 0% -> 32%
where the time goes in v5:
time: 136 us; the launch traced here: 133 us
  Pallas kernels  109 us (80%)
  local copies, waits for them, and re-layouts  17.1 us (13%)
  starting transfers between devices  4.38 us (3%)
  other arithmetic  1.99 us (1%)
    pallas_call x1, Pallas kernels, on_device(): communicate(functools.partial(middle_kernel, sizes, probe_scale), 1, [VME...  32.3 us
    pallas_call x1, Pallas kernels, on_device(): communicate(functools.partial(begin_kernel, sizes), 0, [SMEM, HBM, HBM, V...  31.7 us
    pallas_call x1, Pallas kernels, on_device(): communicate(functools.partial(end_kernel, sizes, probe_scale), 2, [VMEM]...  23.3 us
    pallas_call x2, Pallas kernels, run_step(): pl.pallas_call(step_kernel, out_shape=(jax.ShapeDtypeStruct(extended.shap...  21.7 us
    unnamed x24, local copies, waits for them, and re-layouts  12.9 us
    all_to_all x1, starting transfers between devices, on_device(): lax.all_to_all(later.reshape(band_count, CAP, width, width), 'ty', split_...  4.38 us
    gather x1, local copies, waits for them, and re-layouts, on_device(): jnp.take(intensities.reshape(-1, width, width), holder[1] + batch_rows, a...  3.93 us
  transfers between devices with their start and end apart: 1, of which 0 were waited for; matrix products, arithmetic and copies ran while one was open for 0% of the time, Pallas kernels for 32%

profile of v5, /device:TPU:3, one launch (start us, length us, event | category | flops | bytes accessed | tf_op | source)
XLA Modules:
  0.0 133.3 jit_solution(644107923074772954)
XLA Ops:
  0.6 0.9 convert_reduce_fusion
  1.6 0.7 multiply_add_fusion
  2.3 0.1 fusion
  2.4 0.2 select_reduce_fusion.1
  2.6 0.1 concatenate.6
  2.7 0.1 select_n.21
  2.9 1.6 %copy-done.3 = f32[2,512,512]{2,1,0:T(8,128)S(1)} copy-done((f32[2,512,512]{2,1,0:T(8,128)S(1)}, f32[2,512,512]{2,1,0:T(8,128)}, u32[]{:S(2)}) %copy-start.3) | copy-done | bytes 2097176
  4.4 31.7 %shard_map.95 = (f32[24,128,128]{2,1,0:T(8,128)S(1)}, f32[2,640,640]{2,1,0:T(8,128)}, s32[8,8,128]{2,1,0:T(8,128)S(1)}) custom-call(s32[2,24]{1,0:T(2,128)S(1)} %get-tuple-element.24.holder, f32[2,24,128,128]{3,2,1,0:T(8,128)} %intensities.1, f32[2,512,512]{2,1,0:T(8,128)S(1)} %copy-done.3, s32[8,8,128]{2,1,0:T(8,128)S(1)} %pad.4.wants), custom_call_target="tpu_custom_call" | custom-call | tf_op jit(solution)/shard_map/pallas_call | solution.py:584
  36.2 1.1 copy-done.5
  37.3 0.1 reshape.63
  37.4 3.9 %gather_fusion = f32[24,128,128]{2,1,0:T(8,128)} fusion(f32[48,128,128]{2,1,0:T(8,128)} %bitcast.18, s32[1024]{0:T(1024)S(1)} %pad_clamp_fusion), kind=kCustom, calls=%fused_computation | custom fusion | bytes 3145824 | tf_op jit(solution)/shard_map/jit(_take)/gather | solution.py:607
  41.4 4.4 %all-to-all-start = ((f32[8,3,128,128]{3,2,1,0:T(8,128)}), f32[8,3,128,128]{3,2,1,0:T(8,128)}, u32[]{:S(2)}, u32[]{:S(2)}) async-start(f32[8,3,128,128]{3,2,1,0:T(8,128)} %bitcast.19), calls=%async_computation | async-start | bytes 3145728 | tf_op jit(solution)/shard_map/all_to_all | solution.py:611
  45.8 1.4 %copy-done.6 = f32[24,128,128]{2,1,0:T(8,128)S(1)} copy-done((f32[24,128,128]{2,1,0:T(8,128)S(1)}, f32[24,128,128]{2,1,0:T(8,128)}, u32[]{:S(2)}) %copy-start.6) | copy-done | bytes 1572888
  47.2 1.1 copy-done.7
  48.3 1.1 copy-done.9
  49.5 10.5 %shard_map.96 = (f32[2,640,640]{2,1,0:T(8,128)S(1)}, f32[256,128]{1,0:T(8,128)S(1)}) custom-call(s32[24]{0:T(128)S(1)} %get-tuple-element.26.tops, s32[24]{0:T(128)S(1)} %get-tuple-element.25.lefts, f32[2,640,640]{2,1,0:T(8,128)S(1)} %copy-done, f32[2,128,128]{2,1,0:T(8,128)S(1)} %copy-done.4, f32[24,128,128]{2,1,0:T(8,128)S(1)} %copy-done.6, ...), custom_call_target="tpu_custom_call" | custom-call | flops 38654705664 | bytes 8388608 | tf_op jit(solution)/shard_map/pallas_call | solution.py:159
  60.0 1.7 %copy-done.2 = f32[2,640,640]{2,1,0:T(8,128)} copy-done((f32[2,640,640]{2,1,0:T(8,128)}, f32[2,640,640]{2,1,0:T(8,128)S(1)}, u32[]{:S(2)}) %copy-start.2) | copy-done | bytes 3276824
  61.7 32.3 %shard_map.97 = (f32[2,640,640]{2,1,0:T(8,128)S(1)}, f32[2,128,128]{2,1,0:T(8,128)S(1)}) custom-call(f32[2,640,640]{2,1,0:T(8,128)} %copy-done.2, f32[256,128]{1,0:T(8,128)S(1)} %get-tuple-element.16.probe_term, f32[2,640,640]{2,1,0:T(8,128)} %get-tuple-element.13.extended, f32[2,128,128]{2,1,0:T(8,128)S(1)} %copy-done.4), custom_call_target="tpu_custom_call" | custom-call | tf_op jit(solution)/shard_map/pallas_call | solution.py:615
  94.1 1.7 %copy-done.8 = bf16[2,256,768]{2,1,0:T(8,128)(2,1)S(1)} copy-done((bf16[2,256,768]{2,1,0:T(8,128)(2,1)S(1)}, bf16[2,256,768]{2,1,0:T(8,128)(2,1)}, u32[]{:S(2)}) %copy-start.8) | copy-done | bytes 786456
  95.8 1.1 copy-done.10
  96.9 11.1 %shard_map.98 = (f32[2,640,640]{2,1,0:T(8,128)S(1)}, f32[256,128]{1,0:T(8,128)S(1)}) custom-call(s32[24]{0:T(128)S(1)} %get-tuple-element.28.tops, s32[24]{0:T(128)S(1)} %get-tuple-element.27.lefts, f32[2,640,640]{2,1,0:T(8,128)S(1)} %get-tuple-element.17.extended, f32[2,128,128]{2,1,0:T(8,128)S(1)} %get-tuple-element.18.probe, ...), custom_call_target="tpu_custom_call" | custom-call | flops 38654705664 | bytes 8388608 | tf_op jit(solution)/shard_map/pallas_call | solution.py:159
  108.1 23.3 %shard_map.99 = (f32[2,512,512]{2,1,0:T(8,128)S(1)}, f32[2,128,128]{2,1,0:T(8,128)S(1)}) custom-call(f32[2,640,640]{2,1,0:T(8,128)S(1)} %get-tuple-element.20.gradient, f32[256,128]{1,0:T(8,128)S(1)} %get-tuple-element.21.probe_term, f32[2,640,640]{2,1,0:T(8,128)} %copy-done.1, f32[2,128,128]{2,1,0:T(8,128)S(1)} %get-tuple-element.18.probe), custom_call_target="tpu_custom_call" | custom-call | tf_op jit(solution)/shard_map/pallas_call | solution.py:630
  131.3 1.3 copy.25
  132.7 0.7 copy.26
  (26 shorter events, 0.1 us)
Async XLA Ops:
  2.8 1.6 %copy-start.3 = (f32[2,512,512]{2,1,0:T(8,128)S(1)}, f32[2,512,512]{2,1,0:T(8,128)}, u32[]{:S(2)}) copy-start(f32[2,512,512]{2,1,0:T(8,128)} %object_field.1) | copy-start | bytes 6291460
  36.2 1.1 copy-start.5
  37.4 8.4 %copy-start = (f32[2,640,640]{2,1,0:T(8,128)S(1)}, f32[2,640,640]{2,1,0:T(8,128)}, u32[]{:S(2)}) copy-start(f32[2,640,640]{2,1,0:T(8,128)} %get-tuple-element.13.extended) | copy-start | bytes 9830404
  41.4 4.4 %copy-start.4 = (f32[2,128,128]{2,1,0:T(8,128)S(1)}, f32[2,128,128]{2,1,0:T(8,128)}, u32[]{:S(2)}) copy-start(f32[2,128,128]{2,1,0:T(8,128)} %probe.3) | copy-start | bytes 393220
  41.4 52.7 %all-to-all-start = ((f32[8,3,128,128]{3,2,1,0:T(8,128)}), f32[8,3,128,128]{3,2,1,0:T(8,128)}, u32[]{:S(2)}, u32[]{:S(2)}) async-start(f32[8,3,128,128]{3,2,1,0:T(8,128)} %bitcast.19), calls=%async_computation | async-start | bytes 3145728 | tf_op jit(solution)/shard_map/all_to_all | solution.py:611
  45.8 1.4 %copy-start.6 = (f32[24,128,128]{2,1,0:T(8,128)S(1)}, f32[24,128,128]{2,1,0:T(8,128)}, u32[]{:S(2)}) copy-start(f32[24,128,128]{2,1,0:T(8,128)} %copy-done.5) | copy-start | bytes 4718596
  47.2 1.1 copy-start.7
  48.3 1.1 copy-start.9
  60.0 1.7 %copy-start.2 = (f32[2,640,640]{2,1,0:T(8,128)}, f32[2,640,640]{2,1,0:T(8,128)S(1)}, u32[]{:S(2)}) copy-start(f32[2,640,640]{2,1,0:T(8,128)S(1)} %get-tuple-element.15.gradient) | copy-start | bytes 9830404
  94.0 14.0 %copy-start.1 = (f32[2,640,640]{2,1,0:T(8,128)}, f32[2,640,640]{2,1,0:T(8,128)S(1)}, u32[]{:S(2)}) copy-start(f32[2,640,640]{2,1,0:T(8,128)S(1)} %get-tuple-element.17.extended) | copy-start | bytes 9830404
  94.1 1.7 %copy-start.8 = (bf16[2,256,768]{2,1,0:T(8,128)(2,1)S(1)}, bf16[2,256,768]{2,1,0:T(8,128)(2,1)}, u32[]{:S(2)}) copy-start(bf16[2,256,768]{2,1,0:T(8,128)(2,1)} %constant.10.clone.left_tables) | copy-start | bytes 2359300
  95.8 1.1 copy-start.10
